TPU v7x, 128 devices: a whole 4x4x4 slice. The times are simulated.
128 devices in a mesh: lat: 4 (over z_hi, core), lon: 32 (over y, z_lo, x).
Axes of the slice: x: 4, y: 4, z: 4 (z_hi: 2, z_lo: 2; z = z_hi * 2 + z_lo), core: 2. Of those that a mesh axis runs over, the one named last changes fastest.
Arguments:
- initial_state: bfloat16 [69, 64, 4096], P(None, 'lat', 'lon'), may hold values from -6 to 6
- background_state: bfloat16 [69, 64, 4096], P(None, 'lat', 'lon'), may hold values from -6 to 6
- background_precision: float32 [69], replicated, may hold values from 0.2 to 2
- conv_weight: bfloat16 [9, 69, 256], replicated, may hold values from -0.25 to 0.25
- conv_bias: float32 [256], replicated, may hold values from -3 to 3
- out_weight: bfloat16 [69, 256], replicated, may hold values from -0.375 to 0.375
- swath_patch: int32 [128, 128], P(('lat', 'lon')), may hold values from 0 to 7
- obs_cell: int32 [128, 128, 128], P(('lat', 'lon')), may hold values from 0 to 17534, as said below
- obs_weights: float32 [4, 128, 128, 128], P(None, ('lat', 'lon')), may hold values from 0.05 to 1
- obs_value: float32 [128, 128, 128], P(('lat', 'lon')), may hold values from -6 to 6
- obs_precision: float32 [128, 128, 128], P(('lat', 'lon')), may hold values from 0.3 to 3
Outputs:
- gradient: float32 [69, 64, 4096], P(None, 'lat', 'lon')
- innovation: float32 [128, 128, 128], P(('lat', 'lon'))
Inputs may be any that keep to these rules, and one draw needn't show every extreme that they name: `swath_patch`: entry [t, o] is the patch of tile t, numbered row by row among its 8 patches, in which owner o's observations of slot t lie. `obs_cell`: each entry is channel * 2 * 128 + row * 128 + column of the observation's upper-left neighbouring cell inside its patch, with row below 1 and column below 127.
All inputs are finite; a program needn't handle non-finite values.
Results may differ from a plain program's by a relative error of at most 0.0049.
Values may be sent and summed in bfloat16 or wider, within the bound.
A program may use at most 128 MiB of HBM per device.

v0:
```python
import functools

import jax
import jax.numpy as jnp
from jax import lax
from jax.experimental import pallas as pl
from jax.experimental.pallas import tpu as pltpu
from jax.sharding import PartitionSpec as P

MESH = pl.DeviceIdType.MESH
F32 = jnp.float32
BF16 = jnp.bfloat16
CP = 80
LANES = 128
WIDE = 256
ROOT_HALF = 0.7071067811865476
NORM_DENSITY = 0.3989422804014327
UP, DOWN, LEFT, RIGHT, UL, UR, DL, DR = range(8)
GROUP = 8


def dot(a, b):
    return jnp.dot(a, b, preferred_element_type=F32)


def lane_iota(rows):
    return lax.broadcasted_iota(jnp.int32, (rows, LANES), 1)


def kernel(
    n_lat, n_lon, hid,
    x_ref, wt_ref, wb_ref, wo_ref, wot_ref, bias_ref, swath_ref, cell_ref, w_ref, val_ref, prec_ref,
    cot_ref, innov_ref,
    x32, packed, recv, s1, s2, sobs, slope1, slope2, csend, hcol, hdiag,
    bsc, qsc, inn, inn_recv, hist, ybuf, ubuf, gbuf, brow, bcol, rrow, rdiag, rcol,
    fsend, frecv, bsend, brecv, psend, precv, isend, irecv,
):
    chan, height = x_ref.shape[0], x_ref.shape[1]
    owners = n_lat * n_lon
    chunks = height // 2
    lat = lax.axis_index("lat")
    lon = lax.axis_index("lon")
    me = lat * n_lon + lon
    has_up = lat > 0
    has_down = lat < n_lat - 1
    left = lax.rem(lon + n_lon - 1, n_lon)
    right = lax.rem(lon + 1, n_lon)
    ids = {
        UP: (lat - 1, lon), DOWN: (lat + 1, lon), LEFT: (lat, left), RIGHT: (lat, right),
        UL: (lat - 1, left), UR: (lat - 1, right), DL: (lat + 1, left), DR: (lat + 1, right),
    }
    opposite = {UP: DOWN, DOWN: UP, LEFT: RIGHT, RIGHT: LEFT, UL: DR, DR: UL, UR: DL, DL: UR}

    def coords(k):
        other = lax.rem(me + k, owners)
        return other, (other // n_lon, lax.rem(other, n_lon))

    barrier = pltpu.get_barrier_semaphore()

    def greet(k, carry):
        _, where = coords(k)
        pl.semaphore_signal(barrier, inc=1, device_id=where, device_id_type=MESH)
        return carry

    lax.fori_loop(1, owners, greet, 0)

    x32[pl.ds(chan * height, (CP - chan) * height), :] = jnp.zeros(((CP - chan) * height, LANES), F32)
    x32[pl.ds(0, chan * height), :] = x_ref[...].astype(F32).reshape(chan * height, LANES)
    cell = cell_ref[...]
    packed[pl.ds(0, owners, stride=8), :] = (cell // WIDE).astype(F32)
    packed[pl.ds(1, owners, stride=8), :] = (cell % LANES).astype(F32)
    for k in range(4):
        packed[pl.ds(2 + k, owners, stride=8), :] = w_ref[k]
    packed[pl.ds(6, owners, stride=8), :] = val_ref[...]
    packed[pl.ds(7, owners, stride=8), :] = prec_ref[...]
    zero_rows = jnp.zeros((hid - 3 * CP, (height + 2) * LANES), BF16)
    s1[pl.ds(3 * CP, hid - 3 * CP), :] = zero_rows
    s2[pl.ds(3 * CP, hid - 3 * CP), :] = zero_rows
    lane = lane_iota(CP)
    first_lane = lane == 0
    last_lane = lane == LANES - 1

    def block(r):
        return pl.ds((r + 1) * LANES, LANES)

    for r in range(height):
        s1[pl.ds(CP, CP), block(r)] = x32[pl.ds(r, CP, stride=height), :].astype(BF16)

    def guarded(d):
        if d in (UP, UL, UR):
            return pl.when(has_up)
        if d in (DOWN, DL, DR):
            return pl.when(has_down)
        return lambda f: f()

    def send(src, dst, t, d, sends, recvs):
        copy = pltpu.make_async_remote_copy(
            src_ref=src, dst_ref=dst, send_sem=sends.at[t, d], recv_sem=recvs.at[t, opposite[d]],
            device_id=ids[d], device_id_type=MESH,
        )
        guarded(d)(copy.start)

    def wait_recv(dst, t, d, sends, recvs):
        copy = pltpu.make_async_remote_copy(
            src_ref=dst, dst_ref=dst, send_sem=sends.at[t, d], recv_sem=recvs.at[t, d],
            device_id=ids[d], device_id_type=MESH,
        )
        guarded(d)(copy.wait_recv)

    def wait_send(src, t, d, sends, recvs):
        copy = pltpu.make_async_remote_copy(
            src_ref=src, dst_ref=src, send_sem=sends.at[t, d], recv_sem=recvs.at[t, d],
            device_id=ids[d], device_id_type=MESH,
        )
        guarded(d)(copy.wait_send)

    def column_blocks(rows, first_of, last_of):
        to_left = jnp.zeros((CP, LANES), F32)
        to_right = jnp.zeros((CP, LANES), F32)
        for r in range(rows):
            to_left = jnp.where(lane == r, pltpu.roll(first_of(r), r, 1) if r else first_of(r), to_left)
            to_right = jnp.where(lane == r, pltpu.roll(last_of(r), r + 1, 1), to_right)
        return to_left.astype(BF16), to_right.astype(BF16)

    diag_slots = {UL: 0, UR: 1, DL: 2, DR: 3}

    def centre(s, r):
        return s.at[pl.ds(CP, CP), block(r)]

    def state_sources(s, t):
        return {
            UP: centre(s, 0), UL: centre(s, 0), UR: centre(s, 0),
            DOWN: centre(s, height - 1), DL: centre(s, height - 1), DR: centre(s, height - 1),
            LEFT: csend.at[t, 0], RIGHT: csend.at[t, 1],
        }

    def state_targets(s, t):
        table = {UP: centre(s, -1), DOWN: centre(s, height), LEFT: hcol.at[t, 0], RIGHT: hcol.at[t, 1]}
        for d, slot in diag_slots.items():
            table[d] = hdiag.at[t, slot]
        return table

    def send_state(s, t):
        src, dst = state_sources(s, t), state_targets(s, t)
        for d in (UP, DOWN, UL, UR, DL, DR):
            send(src[d], dst[opposite[d]], t, d, fsend, frecv)

        def row(r):
            return s[pl.ds(CP, CP), block(r)].astype(F32)

        to_left, to_right = column_blocks(height, row, row)
        csend[t, 0] = to_left
        csend[t, 1] = to_right
        for d in (LEFT, RIGHT):
            send(src[d], dst[opposite[d]], t, d, fsend, frecv)

    def receive_state(s, t):
        dst = state_targets(s, t)
        for d in range(8):
            wait_recv(dst[d], t, d, fsend, frecv)
        from_left = hcol[t, 0].astype(F32)
        from_right = hcol[t, 1].astype(F32)
        for r in range(height):
            row = s[pl.ds(CP, CP), block(r)].astype(F32)
            lower = jnp.where(
                first_lane, pltpu.roll(from_left, (LANES - r) % LANES, 1) if r else from_left, pltpu.roll(row, 1, 1)
            )
            upper = jnp.where(last_lane, pltpu.roll(from_right, LANES - 1 - r, 1), pltpu.roll(row, LANES - 1, 1))
            s[pl.ds(0, CP), block(r)] = lower.astype(BF16)
            s[pl.ds(2 * CP, CP), block(r)] = upper.astype(BF16)
        for r, there, a, b in ((-1, has_up, UL, UR), (height, has_down, DL, DR)):

            @pl.when(there)
            def _():
                row = s[pl.ds(CP, CP), block(r)].astype(F32)
                lower = jnp.where(last_lane, hdiag[t, diag_slots[a]].astype(F32), row)
                upper = jnp.where(first_lane, hdiag[t, diag_slots[b]].astype(F32), row)
                s[pl.ds(0, CP), block(r)] = pltpu.roll(lower, 1, 1).astype(BF16)
                s[pl.ds(2 * CP, CP), block(r)] = pltpu.roll(upper, LANES - 1, 1).astype(BF16)

            @pl.when(jnp.logical_not(there))
            def _():
                s[pl.ds(0, 3 * CP), block(r)] = jnp.zeros((3 * CP, LANES), BF16)

    def forward_chunk(s, n, slope):
        pre = bias_ref[...]
        for i in range(3):
            pre = pre + dot(wt_ref[i], s[:, pl.ds((2 * n + i) * LANES, WIDE)])
        cdf = 0.5 * (1.0 + lax.erf(pre * ROOT_HALF))
        slope[:, pl.ds(n * WIDE, WIDE)] = cdf + pre * jnp.exp(-0.5 * pre * pre) * NORM_DENSITY
        update = dot(wo_ref[...], (pre * cdf).astype(BF16))
        return (s[pl.ds(CP, CP), pl.ds((2 * n + 1) * LANES, WIDE)].astype(F32) + update).astype(BF16)

    pl.semaphore_wait(barrier, owners - 1)
    send_state(s1, 0)

    def post(k, carry):
        other, where = coords(k)
        pltpu.make_async_remote_copy(
            src_ref=packed.at[pl.ds(pl.multiple_of(other * 8, 8), 8)],
            dst_ref=recv.at[pl.ds(pl.multiple_of(me * 8, 8), 8)],
            send_sem=psend, recv_sem=precv, device_id=where, device_id_type=MESH,
        ).start()
        return carry

    lax.fori_loop(1, owners, post, 0)
    mine = pl.ds(pl.multiple_of(me * 8, 8), 8)
    recv[mine, :] = packed[mine, :]

    receive_state(s1, 0)
    for n in range(chunks):
        s2[pl.ds(CP, CP), pl.ds((2 * n + 1) * LANES, WIDE)] = forward_chunk(s1, n, slope1)
    send_state(s2, 1)
    receive_state(s2, 1)
    for n in range(chunks):
        sobs[n] = forward_chunk(s2, n, slope2)

    others = pl.ds(0, (owners - 1) * 8)
    pltpu.make_async_remote_copy(
        src_ref=packed.at[others], dst_ref=recv.at[others], send_sem=psend, recv_sem=precv,
        device_id=ids[RIGHT], device_id_type=MESH,
    ).wait()
    column = lax.broadcasted_iota(jnp.int32, (LANES, LANES), 0).astype(F32)
    channel = lax.broadcasted_iota(jnp.int32, (CP, LANES), 0).astype(F32)

    def estimate(group, carry):
        for u in range(GROUP):
            k = group * GROUP + u
            other, _ = coords(k + 1)
            packet = recv[pl.ds(pl.multiple_of(other * 8, 8), 8), :]
            here, after = column == packet[1:2], column == packet[1:2] + 1.0
            table = jnp.concatenate(
                [
                    jnp.where(here, packet[2:3], jnp.where(after, packet[3:4], 0.0)),
                    jnp.where(here, packet[4:5], jnp.where(after, packet[5:6], 0.0)),
                ],
                axis=0,
            ).astype(BF16)
            bsc[k] = table
            picked = channel == packet[0:1]
            found = dot(sobs[swath_ref[0, other]], table)
            gap = jnp.sum(jnp.where(picked, found, 0.0), axis=0, keepdims=True) - packet[6:7]
            inn[other] = gap
            qsc[k] = jnp.where(picked, packet[7:8] * gap, 0.0).astype(BF16)
        return carry

    lax.fori_loop(0, owners // GROUP, estimate, 0)
    hist[0] = jnp.zeros((CP, WIDE), F32)

    def pull(group, last):
        for u in range(GROUP):
            k = group * GROUP + u
            other, where = coords(k + 1)
            copy = pltpu.make_async_remote_copy(
                src_ref=inn.at[other], dst_ref=inn_recv.at[me], send_sem=isend, recv_sem=irecv,
                device_id=where, device_id_type=MESH,
            )
            if u < GROUP - 1:
                copy.start()
            else:
                pl.when(k < owners - 1)(copy.start)
            spot = swath_ref[0, other]
            before = sum(jnp.where(spot == m, last[m], 0) for m in range(chunks))
            share = lax.dot_general(qsc[k], bsc[k], (((1,), (1,)), ((), ())), preferred_element_type=F32)
            hist[k + 1] = hist[before] + share
            last = tuple(jnp.where(spot == m, k + 1, last[m]) for m in range(chunks))
        return last

    last = lax.fori_loop(0, owners // GROUP, pull, (jnp.int32(0),) * chunks)
    inn_recv[me] = inn[me]

    def tap(i, j, r):
        return ybuf[pl.ds((3 * (i + 1) + j + 1) * CP, CP), pl.ds(r * LANES, LANES)]

    def summed(j, r):
        total = None
        for i in (-1, 0, 1):
            if 0 <= r - i < height:
                part = tap(i, j, r - i)
                total = part if total is None else total + part
        return total

    def rim_sources(t):
        return {
            UP: brow.at[t, 0], UL: brow.at[t, 1], UR: brow.at[t, 2],
            DOWN: brow.at[t, 3], DL: brow.at[t, 4], DR: brow.at[t, 5],
            LEFT: bcol.at[t, 0], RIGHT: bcol.at[t, 1],
        }

    def rim_targets(t):
        table = {UP: rrow.at[t, 0], DOWN: rrow.at[t, 1], LEFT: rcol.at[t, 0], RIGHT: rcol.at[t, 1]}
        for d, slot in diag_slots.items():
            table[d] = rdiag.at[t, slot]
        return table

    pad = jnp.zeros((LANES - CP, WIDE), BF16)

    def backward_step(t, cotangent, slope, finish):
        src, dst = rim_sources(t), rim_targets(t)
        for n in range(chunks):
            rounded = jnp.concatenate([cotangent(n).astype(BF16), pad], axis=0)
            spread = (dot(wot_ref[...], rounded) * slope[:, pl.ds(n * WIDE, WIDE)]).astype(BF16)
            ybuf[:, pl.ds(n * WIDE, WIDE)] = dot(wb_ref[...], spread)

        def inner(t_low, t_mid, t_high):
            return (
                t_mid
                + jnp.where(first_lane, 0.0, pltpu.roll(t_high, 1, 1))
                + jnp.where(last_lane, 0.0, pltpu.roll(t_low, LANES - 1, 1))
            )

        for r, at in ((-1, 0), (height, 3)):
            t_low, t_mid, t_high = (summed(j, r) for j in (-1, 0, 1))
            brow[t, at] = inner(t_low, t_mid, t_high).astype(BF16)
            brow[t, at + 1] = t_low.astype(BF16)
            brow[t, at + 2] = t_high.astype(BF16)
        for d in (UP, DOWN, UL, UR, DL, DR):
            send(src[d], dst[opposite[d]], t, d, bsend, brecv)
        to_left, to_right = column_blocks(height, lambda r: summed(-1, r), lambda r: summed(1, r))
        bcol[t, 0] = to_left
        bcol[t, 1] = to_right
        for d in (LEFT, RIGHT):
            send(src[d], dst[opposite[d]], t, d, bsend, brecv)
        for r in range(height):
            ubuf[:, pl.ds(r * LANES, LANES)] = inner(summed(-1, r), summed(0, r), summed(1, r)) + cotangent(r // 2)[
                :, (r % 2) * LANES : (r % 2 + 1) * LANES
            ]
        for d in range(8):
            wait_recv(dst[d], t, d, bsend, brecv)
        for r, there, at, a, b in ((0, has_up, 0, UL, UR), (height - 1, has_down, 1, DL, DR)):

            @pl.when(there)
            def _():
                ubuf[:, pl.ds(r * LANES, LANES)] = (
                    ubuf[:, pl.ds(r * LANES, LANES)]
                    + rrow[t, at].astype(F32)
                    + jnp.where(first_lane, pltpu.roll(rdiag[t, diag_slots[a]].astype(F32), 1, 1), 0.0)
                    + jnp.where(last_lane, pltpu.roll(rdiag[t, diag_slots[b]].astype(F32), LANES - 1, 1), 0.0)
                )

        from_left = rcol[t, 0].astype(F32)
        from_right = rcol[t, 1].astype(F32)
        for r in range(height):
            finish(
                r,
                ubuf[:, pl.ds(r * LANES, LANES)]
                + jnp.where(first_lane, pltpu.roll(from_left, (LANES - r) % LANES, 1) if r else from_left, 0.0)
                + jnp.where(last_lane, pltpu.roll(from_right, LANES - 1 - r, 1), 0.0),
            )

    def keep(r, value):
        gbuf[:, pl.ds(r * LANES, LANES)] = value

    def write(r, value):
        cot_ref[pl.ds(r, chan, stride=height), :] = value[:chan]

    backward_step(0, lambda n: hist[last[n]], slope2, keep)
    backward_step(1, lambda n: gbuf[:, pl.ds(n * WIDE, WIDE)], slope1, write)

    rows = pl.ds(0, owners - 1)
    pltpu.make_async_remote_copy(
        src_ref=inn.at[rows], dst_ref=inn_recv.at[rows], send_sem=isend, recv_sem=irecv,
        device_id=ids[RIGHT], device_id_type=MESH,
    ).wait()
    innov_ref[...] = inn_recv[...].reshape(owners, LANES)
    for t, s in enumerate((s1, s2)):
        src = state_sources(s, t)
        for d in range(8):
            wait_send(src[d], t, d, fsend, frecv)
    for t in range(2):
        src = rim_sources(t)
        for d in range(8):
            wait_send(src[d], t, d, bsend, brecv)


def local(
    n_lat, n_lon,
    initial_state, background_state, background_precision, conv_weight, conv_bias, out_weight,
    swath_patch, obs_cell, obs_weights, obs_value, obs_precision,
):
    chan, height, breadth = initial_state.shape
    hid = conv_weight.shape[2]
    owners = n_lat * n_lon
    chunks = height // 2
    cells = height * breadth
    padded = jnp.pad(conv_weight, ((0, 0), (0, CP - chan), (0, 0)))
    wb = padded.reshape(9 * CP, hid)
    wt = jnp.transpose(jnp.pad(padded.reshape(3, 3 * CP, hid), ((0, 0), (0, hid - 3 * CP), (0, 0))), (0, 2, 1))
    wo = jnp.pad(out_weight, ((0, CP - chan), (0, 0)))
    wot = jnp.transpose(jnp.pad(out_weight, ((0, LANES - chan), (0, 0))))
    vmem = pl.BlockSpec(memory_space=pltpu.VMEM)
    smem = pl.BlockSpec(memory_space=pltpu.SMEM)
    dma = pltpu.SemaphoreType.DMA
    cot, innov = pl.pallas_call(
        functools.partial(kernel, n_lat, n_lon, hid),
        out_shape=(
            jax.ShapeDtypeStruct((chan * height, LANES), F32),
            jax.ShapeDtypeStruct((owners, LANES), F32),
        ),
        in_specs=[vmem] * 6 + [smem] + [vmem] * 4,
        out_specs=(vmem, vmem),
        scratch_shapes=[
            pltpu.VMEM((CP * height, LANES), F32),
            pltpu.VMEM((owners * 8, LANES), F32),
            pltpu.VMEM((owners * 8, LANES), F32),
            pltpu.VMEM((hid, (height + 2) * LANES), BF16),
            pltpu.VMEM((hid, (height + 2) * LANES), BF16),
            pltpu.VMEM((chunks, CP, WIDE), BF16),
            pltpu.VMEM((hid, cells), F32),
            pltpu.VMEM((hid, cells), F32),
            pltpu.VMEM((2, 2, CP, LANES), BF16),
            pltpu.VMEM((2, 2, CP, LANES), BF16),
            pltpu.VMEM((2, 4, CP, LANES), BF16),
            pltpu.VMEM((owners, WIDE, LANES), BF16),
            pltpu.VMEM((owners, CP, LANES), BF16),
            pltpu.VMEM((owners, 1, LANES), F32),
            pltpu.VMEM((owners, 1, LANES), F32),
            pltpu.VMEM((owners + 1, CP, WIDE), F32),
            pltpu.VMEM((9 * CP, cells), F32),
            pltpu.VMEM((CP, cells), F32),
            pltpu.VMEM((CP, cells), F32),
            pltpu.VMEM((2, 6, CP, LANES), BF16),
            pltpu.VMEM((2, 2, CP, LANES), BF16),
            pltpu.VMEM((2, 2, CP, LANES), BF16),
            pltpu.VMEM((2, 4, CP, LANES), BF16),
            pltpu.VMEM((2, 2, CP, LANES), BF16),
            dma((2, 8)), dma((2, 8)), dma((2, 8)), dma((2, 8)),
            dma, dma, dma, dma,
        ],
        compiler_params=pltpu.CompilerParams(
            collective_id=0, has_side_effects=True, vmem_limit_bytes=56 * 1024 * 1024
        ),
    )(
        initial_state, wt, wb, wo, wot, conv_bias[:, None], swath_patch,
        obs_cell[0], obs_weights[:, 0], obs_value[0], obs_precision[0],
    )
    departure = initial_state.astype(F32) - background_state.astype(F32)
    gradient = background_precision[:, None, None] * departure + cot.reshape(chan, height, breadth)
    return gradient, innov[None]


def solution(mesh):
    tile = P(None, "lat", "lon")
    owner = ("lat", "lon")
    in_specs = (
        tile, tile, P(), P(), P(), P(),
        P(owner, None), P(owner, None, None), P(None, owner, None, None), P(owner, None, None), P(owner, None, None),
    )
    return jax.shard_map(
        functools.partial(local, mesh.shape["lat"], mesh.shape["lon"]),
        mesh=mesh, in_specs=in_specs, out_specs=(tile, P(owner, None, None)), check_vma=False,
    )
```

profile of v0, /device:TPU:1, one launch (start us, length us, event | category | flops | bytes accessed | tf_op | source)
XLA Modules:
  0.0 87.4 jit_solution(17253362679131270694)
XLA Ops:
  0.6 0.0 copy-start.2
  0.6 1.4 %pad.18.wo_ref = bf16[80,256]{1,0:T(8,128)(2,1)} pad(bf16[69,256]{1,0:T(8,128)(2,1)} %param.16, bf16[]{:T(256)} %constant.2.clone.1), padding=0_11x0_0 | pad | bytes 76290 | tf_op jit(solution)/shard_map/jit(_pad)/pad | solution.py:389
  2.1 0.9 %copy.15 = bf16[69,256]{0,1:T(8,128)(2,1)S(1)} copy(bf16[69,256]{1,0:T(8,128)(2,1)} %param.16) | data formatting | bytes 70656 | tf_op args[5]
  3.0 0.6 pad_bitcast_fusion.1.wot_ref
  3.6 1.5 %copy.16.bias_ref = f32[256,1]{1,0:T(8,128)} copy(f32[256,1]{0,1:T(1,128)} %bitcast.21) | data formatting | bytes 2048 | tf_op jit(solution)/shard_map/broadcast_in_dim | solution.py:434
  5.1 0.0 copy-done.2
  5.1 0.0 copy-start
  5.1 0.2 copy.14
  5.3 0.6 copy-done
  5.9 0.8 pad_bitcast_fusion.wt_ref
  6.7 0.0 copy-start.1
  6.7 0.0 copy-start.3
  6.7 77.3 %shard_map.122 = (f32[1104,128]{1,0:T(8,128)}, f32[128,128]{1,0:T(8,128)}) custom-call(bf16[69,16,128]{2,1,0:T(8,128)(2,1)} %x_ref.1, bf16[3,256,256]{2,1,0:T(8,128)(2,1)} %pad_bitcast_fusion.wt_ref, bf16[720,256]{1,0:T(8,128)(2,1)} %bitcast.14, bf16[80,256]{1,0:T(8,128)(2,1)} %pad.18.wo_ref, bf16[256,128]{1,0:T(8,128)(2,1)} %pad_bitcast_fusion.1.wot_ref, ...), custom_call_target="tpu_custom_call" | custom-call | tf_op jit(solution)/shard_map/pallas_call | solution.py:394
  84.0 0.0 copy-start.5
  84.0 0.0 copy-done.1
  84.0 0.0 copy-done.3
  84.0 0.6 copy-done.5
  84.7 0.0 copy-start.4
  84.7 2.0 %multiply_add_fusion = f32[69,16,128]{2,1,0:T(8,128)} fusion(f32[69,16,128]{2,1,0:T(8,128)} %bitcast.15, bf16[69,16,128]{2,1,0:T(8,128)(2,1)S(1)} %copy-done.3, bf16[69,16,128]{2,1,0:T(8,128)(2,1)S(1)} %copy-done.1, f32[69]{0:T(128)S(1)} %copy-done.5), kind=kLoop, calls=%fused_computation | loop fusion | flops 706560 | bytes 1696020 | tf_op jit(solution)/shard_map/add | solution.py:438
  86.7 0.0 copy-done.4
  86.7 0.6 copy.18
  (1 shorter events, 0.0 us)
Async XLA Ops:
  0.6 4.5 %copy-start.2 = (bf16[9,69,256]{2,1,0:T(8,128)(2,1)S(1)}, bf16[9,69,256]{2,1,0:T(8,128)(2,1)}, u32[]{:S(2)}) copy-start(bf16[9,69,256]{2,1,0:T(8,128)(2,1)} %param.14) | copy-start | bytes 953860
  5.1 0.7 copy-start
  6.7 77.4 %copy-start.1 = (bf16[69,16,128]{2,1,0:T(8,128)(2,1)S(1)}, bf16[69,16,128]{2,1,0:T(8,128)(2,1)}, u32[]{:S(2)}) copy-start(bf16[69,16,128]{2,1,0:T(8,128)(2,1)} %x_ref.1) | copy-start | bytes 847876
  6.7 77.4 %copy-start.3 = (bf16[69,16,128]{2,1,0:T(8,128)(2,1)S(1)}, bf16[69,16,128]{2,1,0:T(8,128)(2,1)}, u32[]{:S(2)}) copy-start(bf16[69,16,128]{2,1,0:T(8,128)(2,1)} %param.12) | copy-start | bytes 847876
  84.0 0.7 copy-start.5
  84.7 2.1 %copy-start.4 = (f32[128,128]{1,0:T(8,128)S(1)}, f32[128,128]{1,0:T(8,128)}, u32[]{:S(2)}) copy-start(f32[128,128]{1,0:T(8,128)} %get-tuple-element.5) | copy-start | bytes 196612
where the time goes:
time: 87.6 us; the launch traced here: 87.4 us
  Pallas kernels  77.3 us (88%)
  local copies, waits for them, and re-layouts  7.28 us (8%)
  other arithmetic  2.05 us (2%)
    pallas_call x1, Pallas kernels, local(): pl.pallas_call(functools.partial(kernel, n_lat, n_lon, hid), out_shape=(j...  77.3 us
    unnamed x14, local copies, waits for them, and re-layouts  2.73 us
    add x1, other arithmetic, local(): background_precision[:, None, None] * departure  2.05 us

commit v1 on v0

--- a/solution.py
+++ b/solution.py
@@ -29,9 +29,9 @@
 
 def kernel(
     n_lat, n_lon, hid,
-    x_ref, wt_ref, wb_ref, wo_ref, wot_ref, bias_ref, swath_ref, cell_ref, w_ref, val_ref, prec_ref,
-    cot_ref, innov_ref,
-    x32, packed, recv, s1, s2, sobs, slope1, slope2, csend, hcol, hdiag,
+    x_ref, xb_ref, bp_ref, cw_ref, cb_ref, ow_ref, swath_ref, cell_ref, w_ref, val_ref, prec_ref,
+    grad_ref, innov_ref,
+    wpad, wk, wt_ref, wo_ref, wot_ref, x32, packed, recv, s1, s2, sobs, slope1, slope2, csend, hcol, hdiag,
     bsc, qsc, inn, inn_recv, hist, ybuf, ubuf, gbuf, brow, bcol, rrow, rdiag, rcol,
     fsend, frecv, bsend, brecv, psend, precv, isend, irecv,
 ):
@@ -51,19 +51,49 @@
     }
     opposite = {UP: DOWN, DOWN: UP, LEFT: RIGHT, RIGHT: LEFT, UL: DR, DR: UL, UR: DL, DL: UR}
 
-    def coords(k):
-        other = lax.rem(me + k, owners)
-        return other, (other // n_lon, lax.rem(other, n_lon))
-
     barrier = pltpu.get_barrier_semaphore()
 
-    def greet(k, carry):
-        _, where = coords(k)
+    def wrapped(value, count):
+        return value - jnp.where(value >= count, count, 0)
+
+    def to_all(steps, act):
+        for step in steps:
+            there = wrapped(lat + step, n_lat)
+
+            def one(ahead, carry, there=there):
+                column = wrapped(lon + ahead, n_lon)
+                act(there * n_lon + column, (there, column))
+                return carry
+
+            lax.fori_loop(0 if step else 1, n_lon, one, 0, unroll=4 if step else 1)
+
+    def greet(_, where):
         pl.semaphore_signal(barrier, inc=1, device_id=where, device_id_type=MESH)
-        return carry
-
-    lax.fori_loop(1, owners, greet, 0)
-
+
+    to_all(range(n_lat), greet)
+
+    wpad[...] = jnp.zeros((LANES, hid), F32)
+    bias = cb_ref[...]
+    bias_parts = []
+    for _ in range(3):
+        part = bias.astype(BF16).astype(F32)
+        bias_parts.append(part)
+        bias = bias - part
+    spare = lax.broadcasted_iota(jnp.int32, (hid - 3 * CP, hid), 0)
+    bias_rows = jnp.zeros((hid - 3 * CP, hid), F32)
+    for k, part in enumerate(bias_parts):
+        bias_rows = jnp.where(spare == k, part, bias_rows)
+    for i in range(3):
+        for j in range(3):
+            wpad[pl.ds(0, chan), :] = cw_ref[3 * i + j].astype(F32)
+            wk[i, pl.ds(j * CP, CP), :] = wpad[pl.ds(0, CP), :].astype(BF16)
+        wk[i, pl.ds(3 * CP, hid - 3 * CP), :] = (bias_rows if i == 1 else jnp.zeros_like(bias_rows)).astype(BF16)
+        wt_ref[i] = jnp.transpose(wk[i].astype(F32)).astype(BF16)
+    wpad[pl.ds(0, chan), :] = ow_ref[...].astype(F32)
+    wo_ref[...] = wpad[pl.ds(0, CP), :].astype(BF16)
+    wot_ref[...] = jnp.transpose(wpad[...]).astype(BF16)
+    for c in range(chan):
+        grad_ref[pl.ds(c * height, height), :] = bp_ref[0, c] * (x_ref[c].astype(F32) - xb_ref[c].astype(F32))
     x32[pl.ds(chan * height, (CP - chan) * height), :] = jnp.zeros(((CP - chan) * height, LANES), F32)
     x32[pl.ds(0, chan * height), :] = x_ref[...].astype(F32).reshape(chan * height, LANES)
     cell = cell_ref[...]
@@ -73,9 +103,9 @@
         packed[pl.ds(2 + k, owners, stride=8), :] = w_ref[k]
     packed[pl.ds(6, owners, stride=8), :] = val_ref[...]
     packed[pl.ds(7, owners, stride=8), :] = prec_ref[...]
-    zero_rows = jnp.zeros((hid - 3 * CP, (height + 2) * LANES), BF16)
-    s1[pl.ds(3 * CP, hid - 3 * CP), :] = zero_rows
-    s2[pl.ds(3 * CP, hid - 3 * CP), :] = zero_rows
+    ones = jnp.ones((hid - 3 * CP, (height + 2) * LANES), BF16)
+    s1[pl.ds(3 * CP, hid - 3 * CP), :] = ones
+    s2[pl.ds(3 * CP, hid - 3 * CP), :] = ones
     lane = lane_iota(CP)
     first_lane = lane == 0
     last_lane = lane == LANES - 1
@@ -183,9 +213,7 @@
                 s[pl.ds(0, 3 * CP), block(r)] = jnp.zeros((3 * CP, LANES), BF16)
 
     def forward_chunk(s, n, slope):
-        pre = bias_ref[...]
-        for i in range(3):
-            pre = pre + dot(wt_ref[i], s[:, pl.ds((2 * n + i) * LANES, WIDE)])
+        pre = sum(dot(wt_ref[i], s[:, pl.ds((2 * n + i) * LANES, WIDE)]) for i in range(3))
         cdf = 0.5 * (1.0 + lax.erf(pre * ROOT_HALF))
         slope[:, pl.ds(n * WIDE, WIDE)] = cdf + pre * jnp.exp(-0.5 * pre * pre) * NORM_DENSITY
         update = dot(wo_ref[...], (pre * cdf).astype(BF16))
@@ -194,16 +222,14 @@
     pl.semaphore_wait(barrier, owners - 1)
     send_state(s1, 0)
 
-    def post(k, carry):
-        other, where = coords(k)
+    def post(other, where):
         pltpu.make_async_remote_copy(
             src_ref=packed.at[pl.ds(pl.multiple_of(other * 8, 8), 8)],
             dst_ref=recv.at[pl.ds(pl.multiple_of(me * 8, 8), 8)],
             send_sem=psend, recv_sem=precv, device_id=where, device_id_type=MESH,
         ).start()
-        return carry
-
-    lax.fori_loop(1, owners, post, 0)
+
+    to_all(range(n_lat), post)
     mine = pl.ds(pl.multiple_of(me * 8, 8), 8)
     recv[mine, :] = packed[mine, :]
 
@@ -226,8 +252,7 @@
     def estimate(group, carry):
         for u in range(GROUP):
             k = group * GROUP + u
-            other, _ = coords(k + 1)
-            packet = recv[pl.ds(pl.multiple_of(other * 8, 8), 8), :]
+            packet = recv[pl.ds(pl.multiple_of(k * 8, 8), 8), :]
             here, after = column == packet[1:2], column == packet[1:2] + 1.0
             table = jnp.concatenate(
                 [
@@ -238,9 +263,9 @@
             ).astype(BF16)
             bsc[k] = table
             picked = channel == packet[0:1]
-            found = dot(sobs[swath_ref[0, other]], table)
+            found = dot(sobs[swath_ref[0, k]], table)
             gap = jnp.sum(jnp.where(picked, found, 0.0), axis=0, keepdims=True) - packet[6:7]
-            inn[other] = gap
+            inn[k] = gap
             qsc[k] = jnp.where(picked, packet[7:8] * gap, 0.0).astype(BF16)
         return carry
 
@@ -250,16 +275,7 @@
     def pull(group, last):
         for u in range(GROUP):
             k = group * GROUP + u
-            other, where = coords(k + 1)
-            copy = pltpu.make_async_remote_copy(
-                src_ref=inn.at[other], dst_ref=inn_recv.at[me], send_sem=isend, recv_sem=irecv,
-                device_id=where, device_id_type=MESH,
-            )
-            if u < GROUP - 1:
-                copy.start()
-            else:
-                pl.when(k < owners - 1)(copy.start)
-            spot = swath_ref[0, other]
+            spot = swath_ref[0, k]
             before = sum(jnp.where(spot == m, last[m], 0) for m in range(chunks))
             share = lax.dot_general(qsc[k], bsc[k], (((1,), (1,)), ((), ())), preferred_element_type=F32)
             hist[k + 1] = hist[before] + share
@@ -268,6 +284,12 @@
 
     last = lax.fori_loop(0, owners // GROUP, pull, (jnp.int32(0),) * chunks)
     inn_recv[me] = inn[me]
+
+    def give_back(other, where):
+        pltpu.make_async_remote_copy(
+            src_ref=inn.at[other], dst_ref=inn_recv.at[me], send_sem=isend, recv_sem=irecv,
+            device_id=where, device_id_type=MESH,
+        ).start()
 
     def tap(i, j, r):
         return ybuf[pl.ds((3 * (i + 1) + j + 1) * CP, CP), pl.ds(r * LANES, LANES)]
@@ -295,12 +317,13 @@
 
     pad = jnp.zeros((LANES - CP, WIDE), BF16)
 
-    def backward_step(t, cotangent, slope, finish):
+    def backward_step(t, cotangent, slope, meanwhile, finish):
         src, dst = rim_sources(t), rim_targets(t)
         for n in range(chunks):
             rounded = jnp.concatenate([cotangent(n).astype(BF16), pad], axis=0)
             spread = (dot(wot_ref[...], rounded) * slope[:, pl.ds(n * WIDE, WIDE)]).astype(BF16)
-            ybuf[:, pl.ds(n * WIDE, WIDE)] = dot(wb_ref[...], spread)
+            for i in range(3):
+                ybuf[pl.ds(3 * i * CP, 3 * CP), pl.ds(n * WIDE, WIDE)] = dot(wk[i, pl.ds(0, 3 * CP), :], spread)
 
         def inner(t_low, t_mid, t_high):
             return (
@@ -321,6 +344,7 @@
         bcol[t, 1] = to_right
         for d in (LEFT, RIGHT):
             send(src[d], dst[opposite[d]], t, d, bsend, brecv)
+        to_all(meanwhile, give_back)
         for r in range(height):
             ubuf[:, pl.ds(r * LANES, LANES)] = inner(summed(-1, r), summed(0, r), summed(1, r)) + cotangent(r // 2)[
                 :, (r % 2) * LANES : (r % 2 + 1) * LANES
@@ -352,10 +376,11 @@
         gbuf[:, pl.ds(r * LANES, LANES)] = value
 
     def write(r, value):
-        cot_ref[pl.ds(r, chan, stride=height), :] = value[:chan]
-
-    backward_step(0, lambda n: hist[last[n]], slope2, keep)
-    backward_step(1, lambda n: gbuf[:, pl.ds(n * WIDE, WIDE)], slope1, write)
+        here = pl.ds(r, chan, stride=height)
+        grad_ref[here, :] = grad_ref[here, :] + value[:chan]
+
+    backward_step(0, lambda n: hist[last[n]], slope2, range(n_lat - 1), keep)
+    backward_step(1, lambda n: gbuf[:, pl.ds(n * WIDE, WIDE)], slope1, range(n_lat - 1, n_lat), write)
 
     rows = pl.ds(0, owners - 1)
     pltpu.make_async_remote_copy(
@@ -383,23 +408,23 @@
     owners = n_lat * n_lon
     chunks = height // 2
     cells = height * breadth
-    padded = jnp.pad(conv_weight, ((0, 0), (0, CP - chan), (0, 0)))
-    wb = padded.reshape(9 * CP, hid)
-    wt = jnp.transpose(jnp.pad(padded.reshape(3, 3 * CP, hid), ((0, 0), (0, hid - 3 * CP), (0, 0))), (0, 2, 1))
-    wo = jnp.pad(out_weight, ((0, CP - chan), (0, 0)))
-    wot = jnp.transpose(jnp.pad(out_weight, ((0, LANES - chan), (0, 0))))
     vmem = pl.BlockSpec(memory_space=pltpu.VMEM)
     smem = pl.BlockSpec(memory_space=pltpu.SMEM)
     dma = pltpu.SemaphoreType.DMA
-    cot, innov = pl.pallas_call(
+    gradient, innov = pl.pallas_call(
         functools.partial(kernel, n_lat, n_lon, hid),
         out_shape=(
             jax.ShapeDtypeStruct((chan * height, LANES), F32),
             jax.ShapeDtypeStruct((owners, LANES), F32),
         ),
-        in_specs=[vmem] * 6 + [smem] + [vmem] * 4,
+        in_specs=[vmem, vmem, smem, vmem, vmem, vmem, smem] + [vmem] * 4,
         out_specs=(vmem, vmem),
         scratch_shapes=[
+            pltpu.VMEM((LANES, hid), F32),
+            pltpu.VMEM((3, hid, hid), BF16),
+            pltpu.VMEM((3, hid, hid), BF16),
+            pltpu.VMEM((CP, hid), BF16),
+            pltpu.VMEM((hid, LANES), BF16),
             pltpu.VMEM((CP * height, LANES), F32),
             pltpu.VMEM((owners * 8, LANES), F32),
             pltpu.VMEM((owners * 8, LANES), F32),
@@ -431,12 +456,10 @@
             collective_id=0, has_side_effects=True, vmem_limit_bytes=56 * 1024 * 1024
         ),
     )(
-        initial_state, wt, wb, wo, wot, conv_bias[:, None], swath_patch,
+        initial_state, background_state, background_precision[None], conv_weight, conv_bias[None], out_weight, swath_patch,
         obs_cell[0], obs_weights[:, 0], obs_value[0], obs_precision[0],
     )
-    departure = initial_state.astype(F32) - background_state.astype(F32)
-    gradient = background_precision[:, None, None] * departure + cot.reshape(chan, height, breadth)
-    return gradient, innov[None]
+    return gradient.reshape(chan, height, breadth), innov[None]
 
 
 def solution(mesh):

time: 87.6 us -> 64.2 us (0.73)
  Pallas kernels: 77.3 us -> 60.8 us
  local copies, waits for them, and re-layouts: 7.28 us -> 2.56 us
  other arithmetic: 2.05 us -> 0 us
    pallas_call x1, Pallas kernels: 77.3 us -> 60.8 us  [local(): pl.pallas_call(functools.partial(kernel, n_lat, n_lon, hid), out_shape=(j...]
    add x1 -> x0, other arithmetic: 2.05 us -> none  [local(): background_precision[:, None, None] * departure]
    broadcast_in_dim x1 -> x0, local copies, waits for them, and re-layouts: 1.47 us -> none  [local(): conv_bias[:, None]]
    pad x2 -> x0, local copies, waits for them, and re-layouts: 1.46 us -> none  [the longest x1 1.43 us: local(): wo = jnp.pad(out_weight, ((0, CP - chan), (0, 0)))]
    transpose x2 -> x0, local copies, waits for them, and re-layouts: 1.45 us -> none  [the longest x1 0.8 us: local(): jnp.transpose(jnp.pad(padded.reshape(3, 3 * CP, hid), ((0, 0), (0, hid -...]
    unnamed x14 -> x4, local copies, waits for them, and re-layouts: 2.73 us -> 2.56 us
where the time goes in v1:
time: 64.2 us; the launch traced here: 64.1 us
  Pallas kernels  60.8 us (95%)
  local copies, waits for them, and re-layouts  2.56 us (4%)
  between operations  0.65 us (1%)
    pallas_call x1, Pallas kernels, local(): pl.pallas_call(functools.partial(kernel, n_lat, n_lon, hid), out_shape=(j...  60.8 us
    unnamed x4, local copies, waits for them, and re-layouts  2.56 us

profile of v1, /device:TPU:1, one launch (start us, length us, event | category | flops | bytes accessed | tf_op | source)
XLA Modules:
  0.0 64.1 jit_solution(5493548931135882406)
XLA Ops:
  0.6 60.8 %shard_map.122 = (f32[1104,128]{1,0:T(8,128)}, f32[128,128]{1,0:T(8,128)}) custom-call(bf16[69,16,128]{2,1,0:T(8,128)(2,1)} %x_ref.1, bf16[69,16,128]{2,1,0:T(8,128)(2,1)} %xb_ref.1, f32[1,69]{1,0:T(1,128)} %bitcast.15, bf16[9,69,256]{2,1,0:T(8,128)(2,1)} %cw_ref.1, f32[1,256]{1,0:T(1,128)} %bitcast.14, bf16[69,256]{1,0:T(8,128)(2,1)} %ow_ref.1, ...), custom_call_target="tpu_custom_call" | custom-call | tf_op jit(solution)/shard_map/pallas_call | solution.py:414
  61.5 0.0 copy-start
  61.5 1.9 %copy.15 = f32[69,16,128]{2,1,0:T(8,128)} copy(f32[69,16,128]{2,1,0:T(8,128)} %bitcast.8) | data formatting | bytes 1130496
  63.4 0.0 copy-done
  63.4 0.6 copy.16
Async XLA Ops:
  61.5 1.9 %copy-start = (f32[128,128]{1,0:T(8,128)S(1)}, f32[128,128]{1,0:T(8,128)}, u32[]{:S(2)}) copy-start(f32[128,128]{1,0:T(8,128)} %get-tuple-element.5) | copy-start | bytes 196612

commit v2 on v1

--- a/solution.py
+++ b/solution.py
@@ -16,7 +16,7 @@
 ROOT_HALF = 0.7071067811865476
 NORM_DENSITY = 0.3989422804014327
 UP, DOWN, LEFT, RIGHT, UL, UR, DL, DR = range(8)
-GROUP = 8
+GROUP = 16
 
 
 def dot(a, b):
@@ -29,11 +29,11 @@
 
 def kernel(
     n_lat, n_lon, hid,
-    x_ref, xb_ref, bp_ref, cw_ref, cb_ref, ow_ref, swath_ref, cell_ref, w_ref, val_ref, prec_ref,
+    x_hbm, xb_hbm, bp_ref, cw_ref, cb_ref, ow_ref, swath_ref, cell_hbm, w_hbm, val_hbm, prec_hbm,
     grad_ref, innov_ref,
-    wpad, wk, wt_ref, wo_ref, wot_ref, x32, packed, recv, s1, s2, sobs, slope1, slope2, csend, hcol, hdiag,
+    x_ref, xb_ref, cell_ref, w_ref, val_ref, prec_ref, wpad, wk, wt_ref, wo_ref, wot_ref, x32, packed, recv, s1, s2, se, sobs, slope1, slope2, csend, hcol,
     bsc, qsc, inn, inn_recv, hist, ybuf, ubuf, gbuf, brow, bcol, rrow, rdiag, rcol,
-    fsend, frecv, bsend, brecv, psend, precv, isend, irecv,
+    fsend, frecv, bsend, brecv, psend, precv, isend, irecv, loaded,
 ):
     chan, height = x_ref.shape[0], x_ref.shape[1]
     owners = n_lat * n_lon
@@ -70,8 +70,32 @@
     def greet(_, where):
         pl.semaphore_signal(barrier, inc=1, device_id=where, device_id_type=MESH)
 
+    loads = [
+        pltpu.make_async_copy(src, dst, loaded.at[k])
+        for k, (src, dst) in enumerate(
+            (
+                (x_hbm, x_ref), (xb_hbm, xb_ref), (cell_hbm, cell_ref),
+                (w_hbm, w_ref), (val_hbm, val_ref), (prec_hbm, prec_ref),
+            )
+        )
+    ]
+    for load in loads:
+        load.start()
     to_all(range(n_lat), greet)
 
+    x32[pl.ds(chan * height, (CP - chan) * height), :] = jnp.zeros(((CP - chan) * height, LANES), F32)
+    for load in loads:
+        load.wait()
+    for c in range(chan):
+        grad_ref[pl.ds(c * height, height), :] = bp_ref[0, c] * (x_ref[c].astype(F32) - xb_ref[c].astype(F32))
+    x32[pl.ds(0, chan * height), :] = x_ref[...].astype(F32).reshape(chan * height, LANES)
+    cell = cell_ref[...]
+    packed[pl.ds(0, owners, stride=8), :] = (cell // WIDE).astype(F32)
+    packed[pl.ds(1, owners, stride=8), :] = (cell % LANES).astype(F32)
+    for k in range(4):
+        packed[pl.ds(2 + k, owners, stride=8), :] = w_ref[k]
+    packed[pl.ds(6, owners, stride=8), :] = val_ref[...]
+    packed[pl.ds(7, owners, stride=8), :] = prec_ref[...]
     wpad[...] = jnp.zeros((LANES, hid), F32)
     bias = cb_ref[...]
     bias_parts = []
@@ -92,29 +116,36 @@
     wpad[pl.ds(0, chan), :] = ow_ref[...].astype(F32)
     wo_ref[...] = wpad[pl.ds(0, CP), :].astype(BF16)
     wot_ref[...] = jnp.transpose(wpad[...]).astype(BF16)
-    for c in range(chan):
-        grad_ref[pl.ds(c * height, height), :] = bp_ref[0, c] * (x_ref[c].astype(F32) - xb_ref[c].astype(F32))
-    x32[pl.ds(chan * height, (CP - chan) * height), :] = jnp.zeros(((CP - chan) * height, LANES), F32)
-    x32[pl.ds(0, chan * height), :] = x_ref[...].astype(F32).reshape(chan * height, LANES)
-    cell = cell_ref[...]
-    packed[pl.ds(0, owners, stride=8), :] = (cell // WIDE).astype(F32)
-    packed[pl.ds(1, owners, stride=8), :] = (cell % LANES).astype(F32)
-    for k in range(4):
-        packed[pl.ds(2 + k, owners, stride=8), :] = w_ref[k]
-    packed[pl.ds(6, owners, stride=8), :] = val_ref[...]
-    packed[pl.ds(7, owners, stride=8), :] = prec_ref[...]
-    ones = jnp.ones((hid - 3 * CP, (height + 2) * LANES), BF16)
-    s1[pl.ds(3 * CP, hid - 3 * CP), :] = ones
-    s2[pl.ds(3 * CP, hid - 3 * CP), :] = ones
+    def ones(breadth):
+        return jnp.ones((hid - 3 * CP, breadth), BF16)
+
+    s1[pl.ds(3 * CP, hid - 3 * CP), :] = ones((height + 4) * LANES)
+    s2[pl.ds(3 * CP, hid - 3 * CP), :] = ones((height + 2) * LANES)
+    for i in range(3):
+        se[i, pl.ds(3 * CP, hid - 3 * CP), :] = ones(LANES)
     lane = lane_iota(CP)
     first_lane = lane == 0
     last_lane = lane == LANES - 1
 
-    def block(r):
-        return pl.ds((r + 1) * LANES, LANES)
-
+    def block(rim, r, count=1):
+        return pl.ds((r + rim) * LANES, count * LANES)
+
+    def rolled(value, shift):
+        return pltpu.roll(value, shift % LANES, 1) if shift % LANES else value
+
+    def spot(r):
+        return 2 * (r + 2)
+
+    pair_of = lane // 2
+    to_left = jnp.zeros((CP, LANES), F32)
+    to_right = jnp.zeros((CP, LANES), F32)
     for r in range(height):
-        s1[pl.ds(CP, CP), block(r)] = x32[pl.ds(r, CP, stride=height), :].astype(BF16)
+        row = x32[pl.ds(r, CP, stride=height), :]
+        s1[pl.ds(CP, CP), block(2, r)] = row.astype(BF16)
+        to_left = jnp.where(pair_of == r + 2, rolled(row, spot(r)), to_left)
+        to_right = jnp.where(pair_of == r + 2, rolled(row, spot(r) + 2), to_right)
+    csend[0] = to_left.astype(BF16)
+    csend[1] = to_right.astype(BF16)
 
     def guarded(d):
         if d in (UP, UL, UR):
@@ -154,73 +185,96 @@
 
     diag_slots = {UL: 0, UR: 1, DL: 2, DR: 3}
 
-    def centre(s, r):
-        return s.at[pl.ds(CP, CP), block(r)]
-
-    def state_sources(s, t):
-        return {
-            UP: centre(s, 0), UL: centre(s, 0), UR: centre(s, 0),
-            DOWN: centre(s, height - 1), DL: centre(s, height - 1), DR: centre(s, height - 1),
-            LEFT: csend.at[t, 0], RIGHT: csend.at[t, 1],
-        }
-
-    def state_targets(s, t):
-        table = {UP: centre(s, -1), DOWN: centre(s, height), LEFT: hcol.at[t, 0], RIGHT: hcol.at[t, 1]}
-        for d, slot in diag_slots.items():
-            table[d] = hdiag.at[t, slot]
-        return table
-
-    def send_state(s, t):
-        src, dst = state_sources(s, t), state_targets(s, t)
-        for d in (UP, DOWN, UL, UR, DL, DR):
-            send(src[d], dst[opposite[d]], t, d, fsend, frecv)
-
-        def row(r):
-            return s[pl.ds(CP, CP), block(r)].astype(F32)
-
-        to_left, to_right = column_blocks(height, row, row)
-        csend[t, 0] = to_left
-        csend[t, 1] = to_right
-        for d in (LEFT, RIGHT):
-            send(src[d], dst[opposite[d]], t, d, fsend, frecv)
-
-    def receive_state(s, t):
-        dst = state_targets(s, t)
+    def pair(r):
+        return s1.at[pl.ds(CP, CP), block(2, r, 2)]
+
+    state_sources = {
+        UP: pair(0), DOWN: pair(height - 2),
+        LEFT: csend.at[0], UL: csend.at[0], DL: csend.at[0],
+        RIGHT: csend.at[1], UR: csend.at[1], DR: csend.at[1],
+    }
+    state_targets = {UP: pair(-2), DOWN: pair(height)}
+    for k, d in enumerate((LEFT, RIGHT, UL, UR, DL, DR)):
+        state_targets[d] = hcol.at[k]
+
+    def send_state():
+        for d in (UP, DOWN, LEFT, RIGHT, UL, UR, DL, DR):
+            send(state_sources[d], state_targets[opposite[d]], 0, d, fsend, frecv)
+
+    def receive_state():
         for d in range(8):
-            wait_recv(dst[d], t, d, fsend, frecv)
-        from_left = hcol[t, 0].astype(F32)
-        from_right = hcol[t, 1].astype(F32)
-        for r in range(height):
-            row = s[pl.ds(CP, CP), block(r)].astype(F32)
-            lower = jnp.where(
-                first_lane, pltpu.roll(from_left, (LANES - r) % LANES, 1) if r else from_left, pltpu.roll(row, 1, 1)
-            )
-            upper = jnp.where(last_lane, pltpu.roll(from_right, LANES - 1 - r, 1), pltpu.roll(row, LANES - 1, 1))
-            s[pl.ds(0, CP), block(r)] = lower.astype(BF16)
-            s[pl.ds(2 * CP, CP), block(r)] = upper.astype(BF16)
-        for r, there, a, b in ((-1, has_up, UL, UR), (height, has_down, DL, DR)):
-
-            @pl.when(there)
-            def _():
-                row = s[pl.ds(CP, CP), block(r)].astype(F32)
-                lower = jnp.where(last_lane, hdiag[t, diag_slots[a]].astype(F32), row)
-                upper = jnp.where(first_lane, hdiag[t, diag_slots[b]].astype(F32), row)
-                s[pl.ds(0, CP), block(r)] = pltpu.roll(lower, 1, 1).astype(BF16)
-                s[pl.ds(2 * CP, CP), block(r)] = pltpu.roll(upper, LANES - 1, 1).astype(BF16)
+            wait_recv(state_targets[d], 0, d, fsend, frecv)
+        for there, r, slots in ((has_up, -2, (2, 3)), (has_down, height, (4, 5))):
 
             @pl.when(jnp.logical_not(there))
             def _():
-                s[pl.ds(0, 3 * CP), block(r)] = jnp.zeros((3 * CP, LANES), BF16)
-
-    def forward_chunk(s, n, slope):
-        pre = sum(dot(wt_ref[i], s[:, pl.ds((2 * n + i) * LANES, WIDE)]) for i in range(3))
+                s1[pl.ds(CP, CP), block(2, r, 2)] = jnp.zeros((CP, WIDE), BF16)
+                for slot in slots:
+                    hcol[slot] = jnp.zeros((CP, LANES), BF16)
+
+    def shift_rows(s, rim, rows, low, low_lane, high, high_lane):
+        for r in rows:
+            row = s[pl.ds(CP, CP), block(rim, r)].astype(F32)
+            lower = jnp.where(first_lane, rolled(low, -low_lane(r)), rolled(row, 1))
+            upper = jnp.where(last_lane, rolled(high, LANES - 1 - high_lane(r)), rolled(row, -1))
+            s[pl.ds(0, CP), block(rim, r)] = lower.astype(BF16)
+            s[pl.ds(2 * CP, CP), block(rim, r)] = upper.astype(BF16)
+
+    def with_corners(side, above, below):
+        middle = jnp.logical_and(pair_of >= 2, pair_of < height + 2)
+        outer = jnp.where(pair_of < 2, rolled(above, -2 * height), rolled(below, 2 * height))
+        return jnp.where(middle, side, outer)
+
+    def spread_columns():
+        from_left, from_right, ul, ur, dl, dr = (hcol[k].astype(F32) for k in range(6))
+        low = with_corners(from_left, ul, dl)
+        high = with_corners(from_right, ur, dr)
+        first = csend[0].astype(F32)
+        last = rolled(csend[1].astype(F32), -1)
+        for r in (-2, -1, height, height + 1):
+            row = s1[pl.ds(CP, CP), block(2, r)].astype(F32)
+            first = jnp.where(lane == spot(r), rolled(row, spot(r)), first)
+            last = jnp.where(lane == spot(r), rolled(row, spot(r) + 1), last)
+        on_left = lane < LANES // 2
+        taps = (
+            jnp.where(on_left, low, rolled(last, LANES // 2)),
+            jnp.where(on_left, rolled(low, -1), rolled(high, LANES // 2)),
+            jnp.where(on_left, first, rolled(high, LANES // 2 - 1)),
+        )
+        for i in range(3):
+            for j in range(3):
+                se[i, pl.ds(j * CP, CP), :] = rolled(taps[j], 2 * (1 - i)).astype(BF16)
+        return low, high, taps[1]
+
+    def network(window, centre):
+        pre = sum(dot(wt_ref[i], window(i)) for i in range(3))
         cdf = 0.5 * (1.0 + lax.erf(pre * ROOT_HALF))
-        slope[:, pl.ds(n * WIDE, WIDE)] = cdf + pre * jnp.exp(-0.5 * pre * pre) * NORM_DENSITY
         update = dot(wo_ref[...], (pre * cdf).astype(BF16))
-        return (s[pl.ds(CP, CP), pl.ds((2 * n + 1) * LANES, WIDE)].astype(F32) + update).astype(BF16)
+        return centre.astype(F32) + update, lambda: cdf + pre * jnp.exp(-0.5 * pre * pre) * NORM_DENSITY
+
+    def forward_chunk(s, rim, n, slope):
+        state, tangent = network(
+            lambda i: s[:, block(rim, 2 * n + i - 1, 2)], s[pl.ds(CP, CP), block(rim, 2 * n, 2)]
+        )
+        slope[:, pl.ds(n * WIDE, WIDE)] = tangent()
+        return state.astype(BF16)
+
+    def first_rim(centre):
+        up, down = has_up.astype(F32), has_down.astype(F32)
+        rows = (-1, height)
+        state, _ = network(
+            lambda i: jnp.concatenate([s1[:, block(2, r + i - 1)] for r in rows], axis=1),
+            jnp.concatenate([s1[pl.ds(CP, CP), block(2, r)] for r in rows], axis=1),
+        )
+        s2[pl.ds(CP, CP), block(1, -1)] = (state[:, :LANES] * up).astype(BF16)
+        s2[pl.ds(CP, CP), block(1, height)] = (state[:, LANES:] * down).astype(BF16)
+        sides, _ = network(lambda i: se[i], centre)
+        place = lax.rem(lane, LANES // 2)
+        inside = jnp.where(place == spot(-1), up, jnp.where(place == spot(height), down, 1.0))
+        return (sides * inside).astype(BF16).astype(F32)
 
     pl.semaphore_wait(barrier, owners - 1)
-    send_state(s1, 0)
+    send_state()
 
     def post(other, where):
         pltpu.make_async_remote_copy(
@@ -233,13 +287,15 @@
     mine = pl.ds(pl.multiple_of(me * 8, 8), 8)
     recv[mine, :] = packed[mine, :]
 
-    receive_state(s1, 0)
+    receive_state()
+    low, high, beside = spread_columns()
+    shift_rows(s1, 2, range(-2, height + 2), low, lambda r: spot(r) + 1, high, spot)
     for n in range(chunks):
-        s2[pl.ds(CP, CP), pl.ds((2 * n + 1) * LANES, WIDE)] = forward_chunk(s1, n, slope1)
-    send_state(s2, 1)
-    receive_state(s2, 1)
+        s2[pl.ds(CP, CP), block(1, 2 * n, 2)] = forward_chunk(s1, 2, n, slope1)
+    sides = first_rim(beside)
+    shift_rows(s2, 1, range(-1, height + 1), sides, spot, sides, lambda r: LANES // 2 + spot(r))
     for n in range(chunks):
-        sobs[n] = forward_chunk(s2, n, slope2)
+        sobs[n] = forward_chunk(s2, 1, n, slope2)
 
     others = pl.ds(0, (owners - 1) * 8)
     pltpu.make_async_remote_copy(
@@ -275,11 +331,11 @@
     def pull(group, last):
         for u in range(GROUP):
             k = group * GROUP + u
-            spot = swath_ref[0, k]
-            before = sum(jnp.where(spot == m, last[m], 0) for m in range(chunks))
+            patch = swath_ref[0, k]
+            before = sum(jnp.where(patch == m, last[m], 0) for m in range(chunks))
             share = lax.dot_general(qsc[k], bsc[k], (((1,), (1,)), ((), ())), preferred_element_type=F32)
             hist[k + 1] = hist[before] + share
-            last = tuple(jnp.where(spot == m, k + 1, last[m]) for m in range(chunks))
+            last = tuple(jnp.where(patch == m, k + 1, last[m]) for m in range(chunks))
         return last
 
     last = lax.fori_loop(0, owners // GROUP, pull, (jnp.int32(0),) * chunks)
@@ -388,14 +444,23 @@
         device_id=ids[RIGHT], device_id_type=MESH,
     ).wait()
     innov_ref[...] = inn_recv[...].reshape(owners, LANES)
-    for t, s in enumerate((s1, s2)):
-        src = state_sources(s, t)
-        for d in range(8):
-            wait_send(src[d], t, d, fsend, frecv)
+    for d in range(8):
+        wait_send(state_sources[d], 0, d, fsend, frecv)
     for t in range(2):
         src = rim_sources(t)
         for d in range(8):
             wait_send(src[d], t, d, bsend, brecv)
+
+
+def hand_over(gradient_in, innov_in, gradient_out, innov_out, sems):
+    copies = [
+        pltpu.make_async_copy(gradient_in, gradient_out, sems.at[0]),
+        pltpu.make_async_copy(innov_in, innov_out, sems.at[1]),
+    ]
+    for copy in copies:
+        copy.start()
+    for copy in copies:
+        copy.wait()
 
 
 def local(
@@ -409,6 +474,7 @@
     chunks = height // 2
     cells = height * breadth
     vmem = pl.BlockSpec(memory_space=pltpu.VMEM)
+    hbm = pl.BlockSpec(memory_space=pltpu.HBM)
     smem = pl.BlockSpec(memory_space=pltpu.SMEM)
     dma = pltpu.SemaphoreType.DMA
     gradient, innov = pl.pallas_call(
@@ -417,9 +483,15 @@
             jax.ShapeDtypeStruct((chan * height, LANES), F32),
             jax.ShapeDtypeStruct((owners, LANES), F32),
         ),
-        in_specs=[vmem, vmem, smem, vmem, vmem, vmem, smem] + [vmem] * 4,
+        in_specs=[hbm, hbm, smem, vmem, vmem, vmem, smem] + [hbm] * 4,
         out_specs=(vmem, vmem),
         scratch_shapes=[
+            pltpu.VMEM((chan, height, breadth), BF16),
+            pltpu.VMEM((chan, height, breadth), BF16),
+            pltpu.VMEM((owners, LANES), jnp.int32),
+            pltpu.VMEM((4, owners, LANES), F32),
+            pltpu.VMEM((owners, LANES), F32),
+            pltpu.VMEM((owners, LANES), F32),
             pltpu.VMEM((LANES, hid), F32),
             pltpu.VMEM((3, hid, hid), BF16),
             pltpu.VMEM((3, hid, hid), BF16),
@@ -428,14 +500,14 @@
             pltpu.VMEM((CP * height, LANES), F32),
             pltpu.VMEM((owners * 8, LANES), F32),
             pltpu.VMEM((owners * 8, LANES), F32),
+            pltpu.VMEM((hid, (height + 4) * LANES), BF16),
             pltpu.VMEM((hid, (height + 2) * LANES), BF16),
-            pltpu.VMEM((hid, (height + 2) * LANES), BF16),
+            pltpu.VMEM((3, hid, LANES), BF16),
             pltpu.VMEM((chunks, CP, WIDE), BF16),
             pltpu.VMEM((hid, cells), F32),
             pltpu.VMEM((hid, cells), F32),
-            pltpu.VMEM((2, 2, CP, LANES), BF16),
-            pltpu.VMEM((2, 2, CP, LANES), BF16),
-            pltpu.VMEM((2, 4, CP, LANES), BF16),
+            pltpu.VMEM((2, CP, LANES), BF16),
+            pltpu.VMEM((6, CP, LANES), BF16),
             pltpu.VMEM((owners, WIDE, LANES), BF16),
             pltpu.VMEM((owners, CP, LANES), BF16),
             pltpu.VMEM((owners, 1, LANES), F32),
@@ -449,8 +521,8 @@
             pltpu.VMEM((2, 2, CP, LANES), BF16),
             pltpu.VMEM((2, 4, CP, LANES), BF16),
             pltpu.VMEM((2, 2, CP, LANES), BF16),
-            dma((2, 8)), dma((2, 8)), dma((2, 8)), dma((2, 8)),
-            dma, dma, dma, dma,
+            dma((1, 8)), dma((1, 8)), dma((2, 8)), dma((2, 8)),
+            dma, dma, dma, dma, dma((6,)),
         ],
         compiler_params=pltpu.CompilerParams(
             collective_id=0, has_side_effects=True, vmem_limit_bytes=56 * 1024 * 1024
@@ -459,7 +531,17 @@
         initial_state, background_state, background_precision[None], conv_weight, conv_bias[None], out_weight, swath_patch,
         obs_cell[0], obs_weights[:, 0], obs_value[0], obs_precision[0],
     )
-    return gradient.reshape(chan, height, breadth), innov[None]
+    return pl.pallas_call(
+        hand_over,
+        out_shape=(
+            jax.ShapeDtypeStruct((chan, height, breadth), F32),
+            jax.ShapeDtypeStruct((1, owners, LANES), F32),
+        ),
+        in_specs=[hbm, hbm],
+        out_specs=(hbm, hbm),
+        scratch_shapes=[dma((2,))],
+        compiler_params=pltpu.CompilerParams(vmem_limit_bytes=56 * 1024 * 1024),
+    )(gradient.reshape(chan, height, breadth), innov[None])
 
 
 def solution(mesh):

time: 64.2 us -> 75.8 us (1.18)
  Pallas kernels: 60.8 us -> 74.8 us
  local copies, waits for them, and re-layouts: 2.56 us -> 0 us
    pallas_call x0 -> x1, Pallas kernels: none -> 20.2 us  [local(): pl.pallas_call(hand_over, out_shape=(jax.ShapeDtypeStruct((chan, height,...]
    pallas_call x1, Pallas kernels: 60.8 us -> 54.6 us  [local(): pl.pallas_call(functools.partial(kernel, n_lat, n_lon, hid), out_shape=(j...]
    unnamed x4 -> x0, local copies, waits for them, and re-layouts: 2.56 us -> none
where the time goes in v2:
time: 75.8 us; the launch traced here: 75.6 us
  Pallas kernels  74.8 us (99%)
  between operations  0.8 us (1%)
    pallas_call x1, Pallas kernels, local(): pl.pallas_call(functools.partial(kernel, n_lat, n_lon, hid), out_shape=(j...  54.6 us
    pallas_call x1, Pallas kernels, local(): pl.pallas_call(hand_over, out_shape=(jax.ShapeDtypeStruct((chan, height,...  20.2 us

profile of v2, /device:TPU:1, one launch (start us, length us, event | category | flops | bytes accessed | tf_op | source)
XLA Modules:
  0.0 75.6 jit_solution(4738924814709653681)
XLA Ops:
  0.6 54.6 %shard_map.122 = (f32[1104,128]{1,0:T(8,128)}, f32[128,128]{1,0:T(8,128)}) custom-call(bf16[69,16,128]{2,1,0:T(8,128)(2,1)} %x_hbm.1, bf16[69,16,128]{2,1,0:T(8,128)(2,1)} %xb_hbm.1, f32[1,69]{1,0:T(1,128)} %bitcast.15, bf16[9,69,256]{2,1,0:T(8,128)(2,1)} %cw_ref.1, f32[1,256]{1,0:T(1,128)} %bitcast.14, bf16[69,256]{1,0:T(8,128)(2,1)} %ow_ref.1, ...), custom_call_target="tpu_custom_call" | custom-call | tf_op jit(solution)/shard_map/pallas_call | solution.py:480
  55.2 20.2 %shard_map.123 = (f32[69,16,128]{2,1,0:T(8,128)}, f32[1,128,128]{2,1,0:T(8,128)}) custom-call(f32[69,16,128]{2,1,0:T(8,128)} %bitcast.8, f32[1,128,128]{2,1,0:T(8,128)} %bitcast.13), custom_call_target="tpu_custom_call" | custom-call | tf_op jit(solution)/shard_map/pallas_call | solution.py:534

commit v3 on v2

--- a/solution.py
+++ b/solution.py
@@ -17,6 +17,7 @@
 NORM_DENSITY = 0.3989422804014327
 UP, DOWN, LEFT, RIGHT, UL, UR, DL, DR = range(8)
 GROUP = 16
+PIECES = 3
 
 
 def dot(a, b):
@@ -56,16 +57,12 @@
     def wrapped(value, count):
         return value - jnp.where(value >= count, count, 0)
 
-    def to_all(steps, act):
-        for step in steps:
-            there = wrapped(lat + step, n_lat)
-
-            def one(ahead, carry, there=there):
-                column = wrapped(lon + ahead, n_lon)
-                act(there * n_lon + column, (there, column))
-                return carry
-
-            lax.fori_loop(0 if step else 1, n_lon, one, 0, unroll=4 if step else 1)
+    rounds = [(step, ahead) for step in range(n_lat) for ahead in range(n_lon) if step or ahead]
+
+    def to_some(part, parts, act):
+        for step, ahead in rounds[len(rounds) * part // parts : len(rounds) * (part + 1) // parts]:
+            there, column = wrapped(lat + step, n_lat), wrapped(lon + ahead, n_lon)
+            act(there * n_lon + column, (there, column))
 
     def greet(_, where):
         pl.semaphore_signal(barrier, inc=1, device_id=where, device_id_type=MESH)
@@ -81,14 +78,166 @@
     ]
     for load in loads:
         load.start()
-    to_all(range(n_lat), greet)
+    to_some(0, 1, greet)
 
     x32[pl.ds(chan * height, (CP - chan) * height), :] = jnp.zeros(((CP - chan) * height, LANES), F32)
-    for load in loads:
+    loads[0].wait()
+    x32[pl.ds(0, chan * height), :] = x_ref[...].astype(F32).reshape(chan * height, LANES)
+    lane = lane_iota(CP)
+    first_lane = lane == 0
+    last_lane = lane == LANES - 1
+
+    def block(rim, r, count=1):
+        return pl.ds((r + rim) * LANES, count * LANES)
+
+    def rolled(value, shift):
+        return pltpu.roll(value, shift % LANES, 1) if shift % LANES else value
+
+    def spot(r):
+        return 2 * (r + 2)
+
+    pair_of = lane // 2
+    to_left = jnp.zeros((CP, LANES), F32)
+    to_right = jnp.zeros((CP, LANES), F32)
+    for r in range(height):
+        row = x32[pl.ds(r, CP, stride=height), :]
+        s1[pl.ds(CP, CP), block(2, r)] = row.astype(BF16)
+        to_left = jnp.where(pair_of == r + 2, rolled(row, spot(r)), to_left)
+        to_right = jnp.where(pair_of == r + 2, rolled(row, spot(r) + 2), to_right)
+    csend[0] = to_left.astype(BF16)
+    csend[1] = to_right.astype(BF16)
+
+    def guarded(d):
+        if d in (UP, UL, UR):
+            return pl.when(has_up)
+        if d in (DOWN, DL, DR):
+            return pl.when(has_down)
+        return lambda f: f()
+
+    def send(src, dst, t, d, sends, recvs):
+        copy = pltpu.make_async_remote_copy(
+            src_ref=src, dst_ref=dst, send_sem=sends.at[t, d], recv_sem=recvs.at[t, opposite[d]],
+            device_id=ids[d], device_id_type=MESH,
+        )
+        guarded(d)(copy.start)
+
+    def wait_recv(dst, t, d, sends, recvs):
+        copy = pltpu.make_async_remote_copy(
+            src_ref=dst, dst_ref=dst, send_sem=sends.at[t, d], recv_sem=recvs.at[t, d],
+            device_id=ids[d], device_id_type=MESH,
+        )
+        guarded(d)(copy.wait_recv)
+
+    def wait_send(src, t, d, sends, recvs):
+        copy = pltpu.make_async_remote_copy(
+            src_ref=src, dst_ref=src, send_sem=sends.at[t, d], recv_sem=recvs.at[t, d],
+            device_id=ids[d], device_id_type=MESH,
+        )
+        guarded(d)(copy.wait_send)
+
+    def column_blocks(rows, first_of, last_of):
+        to_left = jnp.zeros((CP, LANES), F32)
+        to_right = jnp.zeros((CP, LANES), F32)
+        for r in range(rows):
+            to_left = jnp.where(lane == r, pltpu.roll(first_of(r), r, 1) if r else first_of(r), to_left)
+            to_right = jnp.where(lane == r, pltpu.roll(last_of(r), r + 1, 1), to_right)
+        return to_left.astype(BF16), to_right.astype(BF16)
+
+    diag_slots = {UL: 0, UR: 1, DL: 2, DR: 3}
+
+    def pair(r):
+        return s1.at[pl.ds(CP, CP), block(2, r, 2)]
+
+    state_sources = {
+        UP: pair(0), DOWN: pair(height - 2),
+        LEFT: csend.at[0], UL: csend.at[0], DL: csend.at[0],
+        RIGHT: csend.at[1], UR: csend.at[1], DR: csend.at[1],
+    }
+    state_targets = {UP: pair(-2), DOWN: pair(height)}
+    for k, d in enumerate((LEFT, RIGHT, UL, UR, DL, DR)):
+        state_targets[d] = hcol.at[k]
+
+    def send_state():
+        for d in (UP, DOWN, LEFT, RIGHT, UL, UR, DL, DR):
+            send(state_sources[d], state_targets[opposite[d]], 0, d, fsend, frecv)
+
+    def receive_state():
+        for d in range(8):
+            wait_recv(state_targets[d], 0, d, fsend, frecv)
+        for there, r, slots in ((has_up, -2, (2, 3)), (has_down, height, (4, 5))):
+
+            @pl.when(jnp.logical_not(there))
+            def _():
+                s1[pl.ds(CP, CP), block(2, r, 2)] = jnp.zeros((CP, WIDE), BF16)
+                for slot in slots:
+                    hcol[slot] = jnp.zeros((CP, LANES), BF16)
+
+    def shift_rows(s, rim, rows, low, low_lane, high, high_lane):
+        for r in rows:
+            row = s[pl.ds(CP, CP), block(rim, r)].astype(F32)
+            lower = jnp.where(first_lane, rolled(low, -low_lane(r)), rolled(row, 1))
+            upper = jnp.where(last_lane, rolled(high, LANES - 1 - high_lane(r)), rolled(row, -1))
+            s[pl.ds(0, CP), block(rim, r)] = lower.astype(BF16)
+            s[pl.ds(2 * CP, CP), block(rim, r)] = upper.astype(BF16)
+
+    def with_corners(side, above, below):
+        middle = jnp.logical_and(pair_of >= 2, pair_of < height + 2)
+        outer = jnp.where(pair_of < 2, rolled(above, -2 * height), rolled(below, 2 * height))
+        return jnp.where(middle, side, outer)
+
+    def spread_columns():
+        from_left, from_right, ul, ur, dl, dr = (hcol[k].astype(F32) for k in range(6))
+        low = with_corners(from_left, ul, dl)
+        high = with_corners(from_right, ur, dr)
+        first = csend[0].astype(F32)
+        last = rolled(csend[1].astype(F32), -1)
+        for r in (-2, -1, height, height + 1):
+            row = s1[pl.ds(CP, CP), block(2, r)].astype(F32)
+            first = jnp.where(lane == spot(r), rolled(row, spot(r)), first)
+            last = jnp.where(lane == spot(r), rolled(row, spot(r) + 1), last)
+        on_left = lane < LANES // 2
+        taps = (
+            jnp.where(on_left, low, rolled(last, LANES // 2)),
+            jnp.where(on_left, rolled(low, -1), rolled(high, LANES // 2)),
+            jnp.where(on_left, first, rolled(high, LANES // 2 - 1)),
+        )
+        for i in range(3):
+            for j in range(3):
+                se[i, pl.ds(j * CP, CP), :] = rolled(taps[j], 2 * (1 - i)).astype(BF16)
+        return low, high, taps[1]
+
+    def network(window, centre):
+        pre = sum(dot(wt_ref[i], window(i)) for i in range(3))
+        cdf = 0.5 * (1.0 + lax.erf(pre * ROOT_HALF))
+        update = dot(wo_ref[...], (pre * cdf).astype(BF16))
+        return centre.astype(F32) + update, lambda: cdf + pre * jnp.exp(-0.5 * pre * pre) * NORM_DENSITY
+
+    def forward_chunk(s, rim, n, slope):
+        state, tangent = network(
+            lambda i: s[:, block(rim, 2 * n + i - 1, 2)], s[pl.ds(CP, CP), block(rim, 2 * n, 2)]
+        )
+        slope[:, pl.ds(n * WIDE, WIDE)] = tangent()
+        return state.astype(BF16)
+
+    def first_rim(centre):
+        up, down = has_up.astype(F32), has_down.astype(F32)
+        rows = (-1, height)
+        state, _ = network(
+            lambda i: jnp.concatenate([s1[:, block(2, r + i - 1)] for r in rows], axis=1),
+            jnp.concatenate([s1[pl.ds(CP, CP), block(2, r)] for r in rows], axis=1),
+        )
+        s2[pl.ds(CP, CP), block(1, -1)] = (state[:, :LANES] * up).astype(BF16)
+        s2[pl.ds(CP, CP), block(1, height)] = (state[:, LANES:] * down).astype(BF16)
+        sides, _ = network(lambda i: se[i], centre)
+        place = lax.rem(lane, LANES // 2)
+        inside = jnp.where(place == spot(-1), up, jnp.where(place == spot(height), down, 1.0))
+        return (sides * inside).astype(BF16).astype(F32)
+
+    pl.semaphore_wait(barrier, owners - 1)
+    send_state()
+
+    for load in loads[1:]:
         load.wait()
-    for c in range(chan):
-        grad_ref[pl.ds(c * height, height), :] = bp_ref[0, c] * (x_ref[c].astype(F32) - xb_ref[c].astype(F32))
-    x32[pl.ds(0, chan * height), :] = x_ref[...].astype(F32).reshape(chan * height, LANES)
     cell = cell_ref[...]
     packed[pl.ds(0, owners, stride=8), :] = (cell // WIDE).astype(F32)
     packed[pl.ds(1, owners, stride=8), :] = (cell % LANES).astype(F32)
@@ -96,6 +245,17 @@
         packed[pl.ds(2 + k, owners, stride=8), :] = w_ref[k]
     packed[pl.ds(6, owners, stride=8), :] = val_ref[...]
     packed[pl.ds(7, owners, stride=8), :] = prec_ref[...]
+
+    def post(other, where):
+        pltpu.make_async_remote_copy(
+            src_ref=packed.at[pl.ds(pl.multiple_of(other * 8, 8), 8)],
+            dst_ref=recv.at[pl.ds(pl.multiple_of(me * 8, 8), 8)],
+            send_sem=psend, recv_sem=precv, device_id=where, device_id_type=MESH,
+        ).start()
+
+    mine = pl.ds(pl.multiple_of(me * 8, 8), 8)
+    recv[mine, :] = packed[mine, :]
+
     wpad[...] = jnp.zeros((LANES, hid), F32)
     bias = cb_ref[...]
     bias_parts = []
@@ -116,6 +276,9 @@
     wpad[pl.ds(0, chan), :] = ow_ref[...].astype(F32)
     wo_ref[...] = wpad[pl.ds(0, CP), :].astype(BF16)
     wot_ref[...] = jnp.transpose(wpad[...]).astype(BF16)
+    for c in range(chan):
+        grad_ref[pl.ds(c * height, height), :] = bp_ref[0, c] * (x_ref[c].astype(F32) - xb_ref[c].astype(F32))
+
     def ones(breadth):
         return jnp.ones((hid - 3 * CP, breadth), BF16)
 
@@ -123,174 +286,12 @@
     s2[pl.ds(3 * CP, hid - 3 * CP), :] = ones((height + 2) * LANES)
     for i in range(3):
         se[i, pl.ds(3 * CP, hid - 3 * CP), :] = ones(LANES)
-    lane = lane_iota(CP)
-    first_lane = lane == 0
-    last_lane = lane == LANES - 1
-
-    def block(rim, r, count=1):
-        return pl.ds((r + rim) * LANES, count * LANES)
-
-    def rolled(value, shift):
-        return pltpu.roll(value, shift % LANES, 1) if shift % LANES else value
-
-    def spot(r):
-        return 2 * (r + 2)
-
-    pair_of = lane // 2
-    to_left = jnp.zeros((CP, LANES), F32)
-    to_right = jnp.zeros((CP, LANES), F32)
-    for r in range(height):
-        row = x32[pl.ds(r, CP, stride=height), :]
-        s1[pl.ds(CP, CP), block(2, r)] = row.astype(BF16)
-        to_left = jnp.where(pair_of == r + 2, rolled(row, spot(r)), to_left)
-        to_right = jnp.where(pair_of == r + 2, rolled(row, spot(r) + 2), to_right)
-    csend[0] = to_left.astype(BF16)
-    csend[1] = to_right.astype(BF16)
-
-    def guarded(d):
-        if d in (UP, UL, UR):
-            return pl.when(has_up)
-        if d in (DOWN, DL, DR):
-            return pl.when(has_down)
-        return lambda f: f()
-
-    def send(src, dst, t, d, sends, recvs):
-        copy = pltpu.make_async_remote_copy(
-            src_ref=src, dst_ref=dst, send_sem=sends.at[t, d], recv_sem=recvs.at[t, opposite[d]],
-            device_id=ids[d], device_id_type=MESH,
-        )
-        guarded(d)(copy.start)
-
-    def wait_recv(dst, t, d, sends, recvs):
-        copy = pltpu.make_async_remote_copy(
-            src_ref=dst, dst_ref=dst, send_sem=sends.at[t, d], recv_sem=recvs.at[t, d],
-            device_id=ids[d], device_id_type=MESH,
-        )
-        guarded(d)(copy.wait_recv)
-
-    def wait_send(src, t, d, sends, recvs):
-        copy = pltpu.make_async_remote_copy(
-            src_ref=src, dst_ref=src, send_sem=sends.at[t, d], recv_sem=recvs.at[t, d],
-            device_id=ids[d], device_id_type=MESH,
-        )
-        guarded(d)(copy.wait_send)
-
-    def column_blocks(rows, first_of, last_of):
-        to_left = jnp.zeros((CP, LANES), F32)
-        to_right = jnp.zeros((CP, LANES), F32)
-        for r in range(rows):
-            to_left = jnp.where(lane == r, pltpu.roll(first_of(r), r, 1) if r else first_of(r), to_left)
-            to_right = jnp.where(lane == r, pltpu.roll(last_of(r), r + 1, 1), to_right)
-        return to_left.astype(BF16), to_right.astype(BF16)
-
-    diag_slots = {UL: 0, UR: 1, DL: 2, DR: 3}
-
-    def pair(r):
-        return s1.at[pl.ds(CP, CP), block(2, r, 2)]
-
-    state_sources = {
-        UP: pair(0), DOWN: pair(height - 2),
-        LEFT: csend.at[0], UL: csend.at[0], DL: csend.at[0],
-        RIGHT: csend.at[1], UR: csend.at[1], DR: csend.at[1],
-    }
-    state_targets = {UP: pair(-2), DOWN: pair(height)}
-    for k, d in enumerate((LEFT, RIGHT, UL, UR, DL, DR)):
-        state_targets[d] = hcol.at[k]
-
-    def send_state():
-        for d in (UP, DOWN, LEFT, RIGHT, UL, UR, DL, DR):
-            send(state_sources[d], state_targets[opposite[d]], 0, d, fsend, frecv)
-
-    def receive_state():
-        for d in range(8):
-            wait_recv(state_targets[d], 0, d, fsend, frecv)
-        for there, r, slots in ((has_up, -2, (2, 3)), (has_down, height, (4, 5))):
-
-            @pl.when(jnp.logical_not(there))
-            def _():
-                s1[pl.ds(CP, CP), block(2, r, 2)] = jnp.zeros((CP, WIDE), BF16)
-                for slot in slots:
-                    hcol[slot] = jnp.zeros((CP, LANES), BF16)
-
-    def shift_rows(s, rim, rows, low, low_lane, high, high_lane):
-        for r in rows:
-            row = s[pl.ds(CP, CP), block(rim, r)].astype(F32)
-            lower = jnp.where(first_lane, rolled(low, -low_lane(r)), rolled(row, 1))
-            upper = jnp.where(last_lane, rolled(high, LANES - 1 - high_lane(r)), rolled(row, -1))
-            s[pl.ds(0, CP), block(rim, r)] = lower.astype(BF16)
-            s[pl.ds(2 * CP, CP), block(rim, r)] = upper.astype(BF16)
-
-    def with_corners(side, above, below):
-        middle = jnp.logical_and(pair_of >= 2, pair_of < height + 2)
-        outer = jnp.where(pair_of < 2, rolled(above, -2 * height), rolled(below, 2 * height))
-        return jnp.where(middle, side, outer)
-
-    def spread_columns():
-        from_left, from_right, ul, ur, dl, dr = (hcol[k].astype(F32) for k in range(6))
-        low = with_corners(from_left, ul, dl)
-        high = with_corners(from_right, ur, dr)
-        first = csend[0].astype(F32)
-        last = rolled(csend[1].astype(F32), -1)
-        for r in (-2, -1, height, height + 1):
-            row = s1[pl.ds(CP, CP), block(2, r)].astype(F32)
-            first = jnp.where(lane == spot(r), rolled(row, spot(r)), first)
-            last = jnp.where(lane == spot(r), rolled(row, spot(r) + 1), last)
-        on_left = lane < LANES // 2
-        taps = (
-            jnp.where(on_left, low, rolled(last, LANES // 2)),
-            jnp.where(on_left, rolled(low, -1), rolled(high, LANES // 2)),
-            jnp.where(on_left, first, rolled(high, LANES // 2 - 1)),
-        )
-        for i in range(3):
-            for j in range(3):
-                se[i, pl.ds(j * CP, CP), :] = rolled(taps[j], 2 * (1 - i)).astype(BF16)
-        return low, high, taps[1]
-
-    def network(window, centre):
-        pre = sum(dot(wt_ref[i], window(i)) for i in range(3))
-        cdf = 0.5 * (1.0 + lax.erf(pre * ROOT_HALF))
-        update = dot(wo_ref[...], (pre * cdf).astype(BF16))
-        return centre.astype(F32) + update, lambda: cdf + pre * jnp.exp(-0.5 * pre * pre) * NORM_DENSITY
-
-    def forward_chunk(s, rim, n, slope):
-        state, tangent = network(
-            lambda i: s[:, block(rim, 2 * n + i - 1, 2)], s[pl.ds(CP, CP), block(rim, 2 * n, 2)]
-        )
-        slope[:, pl.ds(n * WIDE, WIDE)] = tangent()
-        return state.astype(BF16)
-
-    def first_rim(centre):
-        up, down = has_up.astype(F32), has_down.astype(F32)
-        rows = (-1, height)
-        state, _ = network(
-            lambda i: jnp.concatenate([s1[:, block(2, r + i - 1)] for r in rows], axis=1),
-            jnp.concatenate([s1[pl.ds(CP, CP), block(2, r)] for r in rows], axis=1),
-        )
-        s2[pl.ds(CP, CP), block(1, -1)] = (state[:, :LANES] * up).astype(BF16)
-        s2[pl.ds(CP, CP), block(1, height)] = (state[:, LANES:] * down).astype(BF16)
-        sides, _ = network(lambda i: se[i], centre)
-        place = lax.rem(lane, LANES // 2)
-        inside = jnp.where(place == spot(-1), up, jnp.where(place == spot(height), down, 1.0))
-        return (sides * inside).astype(BF16).astype(F32)
-
-    pl.semaphore_wait(barrier, owners - 1)
-    send_state()
-
-    def post(other, where):
-        pltpu.make_async_remote_copy(
-            src_ref=packed.at[pl.ds(pl.multiple_of(other * 8, 8), 8)],
-            dst_ref=recv.at[pl.ds(pl.multiple_of(me * 8, 8), 8)],
-            send_sem=psend, recv_sem=precv, device_id=where, device_id_type=MESH,
-        ).start()
-
-    to_all(range(n_lat), post)
-    mine = pl.ds(pl.multiple_of(me * 8, 8), 8)
-    recv[mine, :] = packed[mine, :]
 
     receive_state()
     low, high, beside = spread_columns()
     shift_rows(s1, 2, range(-2, height + 2), low, lambda r: spot(r) + 1, high, spot)
     for n in range(chunks):
+        to_some(n, chunks, post)
         s2[pl.ds(CP, CP), block(1, 2 * n, 2)] = forward_chunk(s1, 2, n, slope1)
     sides = first_rim(beside)
     shift_rows(s2, 1, range(-1, height + 1), sides, spot, sides, lambda r: LANES // 2 + spot(r))
@@ -302,21 +303,26 @@
         src_ref=packed.at[others], dst_ref=recv.at[others], send_sem=psend, recv_sem=precv,
         device_id=ids[RIGHT], device_id_type=MESH,
     ).wait()
-    column = lax.broadcasted_iota(jnp.int32, (LANES, LANES), 0).astype(F32)
+    column = lax.broadcasted_iota(jnp.int32, (LANES, LANES), 0).astype(F32).astype(BF16)
     channel = lax.broadcasted_iota(jnp.int32, (CP, LANES), 0).astype(F32)
+    zero = jnp.zeros((LANES, LANES), BF16)
 
     def estimate(group, carry):
         for u in range(GROUP):
             k = group * GROUP + u
             packet = recv[pl.ds(pl.multiple_of(k * 8, 8), 8), :]
-            here, after = column == packet[1:2], column == packet[1:2] + 1.0
+            def row(which):
+                return jnp.broadcast_to(packet[which : which + 1].astype(BF16), (LANES, LANES))
+
+            at = row(1)
+            here, after = column == at, column == at + 1
             table = jnp.concatenate(
                 [
-                    jnp.where(here, packet[2:3], jnp.where(after, packet[3:4], 0.0)),
-                    jnp.where(here, packet[4:5], jnp.where(after, packet[5:6], 0.0)),
+                    jnp.where(here, row(2), jnp.where(after, row(3), zero)),
+                    jnp.where(here, row(4), jnp.where(after, row(5), zero)),
                 ],
                 axis=0,
-            ).astype(BF16)
+            )
             bsc[k] = table
             picked = channel == packet[0:1]
             found = dot(sobs[swath_ref[0, k]], table)
@@ -373,7 +379,7 @@
 
     pad = jnp.zeros((LANES - CP, WIDE), BF16)
 
-    def backward_step(t, cotangent, slope, meanwhile, finish):
+    def backward_step(t, cotangent, slope, finish):
         src, dst = rim_sources(t), rim_targets(t)
         for n in range(chunks):
             rounded = jnp.concatenate([cotangent(n).astype(BF16), pad], axis=0)
@@ -400,8 +406,8 @@
         bcol[t, 1] = to_right
         for d in (LEFT, RIGHT):
             send(src[d], dst[opposite[d]], t, d, bsend, brecv)
-        to_all(meanwhile, give_back)
         for r in range(height):
+            to_some(height * t + r, 2 * height, give_back)
             ubuf[:, pl.ds(r * LANES, LANES)] = inner(summed(-1, r), summed(0, r), summed(1, r)) + cotangent(r // 2)[
                 :, (r % 2) * LANES : (r % 2 + 1) * LANES
             ]
@@ -435,8 +441,8 @@
         here = pl.ds(r, chan, stride=height)
         grad_ref[here, :] = grad_ref[here, :] + value[:chan]
 
-    backward_step(0, lambda n: hist[last[n]], slope2, range(n_lat - 1), keep)
-    backward_step(1, lambda n: gbuf[:, pl.ds(n * WIDE, WIDE)], slope1, range(n_lat - 1, n_lat), write)
+    backward_step(0, lambda n: hist[last[n]], slope2, keep)
+    backward_step(1, lambda n: gbuf[:, pl.ds(n * WIDE, WIDE)], slope1, write)
 
     rows = pl.ds(0, owners - 1)
     pltpu.make_async_remote_copy(
@@ -452,15 +458,21 @@
             wait_send(src[d], t, d, bsend, brecv)
 
 
-def hand_over(gradient_in, innov_in, gradient_out, innov_out, sems):
-    copies = [
-        pltpu.make_async_copy(gradient_in, gradient_out, sems.at[0]),
-        pltpu.make_async_copy(innov_in, innov_out, sems.at[1]),
-    ]
-    for copy in copies:
-        copy.start()
-    for copy in copies:
-        copy.wait()
+def hand_over(gradient_in, innov_in, gradient_out, innov_out, gradient_held, innov_held, sems):
+    chan = gradient_in.shape[0]
+    cuts = [chan * k // PIECES for k in range(PIECES + 1)]
+    parts = [pl.ds(a, b - a) for a, b in zip(cuts, cuts[1:])]
+    routes = [(gradient_in.at[p], gradient_held.at[p], gradient_out.at[p]) for p in parts]
+    routes.append((innov_in, innov_held, innov_out))
+    reads = [pltpu.make_async_copy(src, held, sems.at[0, k]) for k, (src, held, _) in enumerate(routes)]
+    writes = [pltpu.make_async_copy(held, dst, sems.at[1, k]) for k, (_, held, dst) in enumerate(routes)]
+    for read in reads:
+        read.start()
+    for read, write in zip(reads, writes):
+        read.wait()
+        write.start()
+    for write in writes:
+        write.wait()
 
 
 def local(
@@ -539,7 +551,11 @@
         ),
         in_specs=[hbm, hbm],
         out_specs=(hbm, hbm),
-        scratch_shapes=[dma((2,))],
+        scratch_shapes=[
+            pltpu.VMEM((chan, height, breadth), F32),
+            pltpu.VMEM((1, owners, LANES), F32),
+            dma((2, PIECES + 1)),
+        ],
         compiler_params=pltpu.CompilerParams(vmem_limit_bytes=56 * 1024 * 1024),
     )(gradient.reshape(chan, height, breadth), innov[None])
 

time: 75.8 us -> 56.4 us (0.74)
  Pallas kernels: 74.8 us -> 55.4 us
    pallas_call x1, Pallas kernels: 20.2 us -> 1.87 us  [local(): pl.pallas_call(hand_over, out_shape=(jax.ShapeDtypeStruct((chan, height,...]
    pallas_call x1, Pallas kernels: 54.6 us -> 53.5 us  [local(): pl.pallas_call(functools.partial(kernel, n_lat, n_lon, hid), out_shape=(j...]
where the time goes in v3:
time: 56.4 us; the launch traced here: 56.2 us
  Pallas kernels  55.4 us (98%)
  between operations  0.8 us (1%)
    pallas_call x1, Pallas kernels, local(): pl.pallas_call(functools.partial(kernel, n_lat, n_lon, hid), out_shape=(j...  53.5 us
    pallas_call x1, Pallas kernels, local(): pl.pallas_call(hand_over, out_shape=(jax.ShapeDtypeStruct((chan, height,...  1.87 us

profile of v3, /device:TPU:1, one launch (start us, length us, event | category | flops | bytes accessed | tf_op | source)
XLA Modules:
  0.0 56.2 jit_solution(1772034590237222888)
XLA Ops:
  0.6 53.5 %shard_map.122 = (f32[1104,128]{1,0:T(8,128)}, f32[128,128]{1,0:T(8,128)}) custom-call(bf16[69,16,128]{2,1,0:T(8,128)(2,1)} %x_hbm.1, bf16[69,16,128]{2,1,0:T(8,128)(2,1)} %xb_hbm.1, f32[1,69]{1,0:T(1,128)} %bitcast.15, bf16[9,69,256]{2,1,0:T(8,128)(2,1)} %cw_ref.1, f32[1,256]{1,0:T(1,128)} %bitcast.14, bf16[69,256]{1,0:T(8,128)(2,1)} %ow_ref.1, ...), custom_call_target="tpu_custom_call" | custom-call | tf_op jit(solution)/shard_map/pallas_call | solution.py:492
  54.2 1.9 %shard_map.123 = (f32[69,16,128]{2,1,0:T(8,128)}, f32[1,128,128]{2,1,0:T(8,128)}) custom-call(f32[69,16,128]{2,1,0:T(8,128)} %bitcast.8, f32[1,128,128]{2,1,0:T(8,128)} %bitcast.13), custom_call_target="tpu_custom_call" | custom-call | tf_op jit(solution)/shard_map/pallas_call | solution.py:546

commit v4 on v3

--- a/solution.py
+++ b/solution.py
@@ -32,8 +32,8 @@
     n_lat, n_lon, hid,
     x_hbm, xb_hbm, bp_ref, cw_ref, cb_ref, ow_ref, swath_ref, cell_hbm, w_hbm, val_hbm, prec_hbm,
     grad_ref, innov_ref,
-    x_ref, xb_ref, cell_ref, w_ref, val_ref, prec_ref, wpad, wk, wt_ref, wo_ref, wot_ref, x32, packed, recv, s1, s2, se, sobs, slope1, slope2, csend, hcol,
-    bsc, qsc, inn, inn_recv, hist, ybuf, ubuf, gbuf, brow, bcol, rrow, rdiag, rcol,
+    x_ref, xb_ref, cell_ref, w_ref, val_ref, prec_ref, wpad, wk, wt_ref, wo_ref, wot_ref, x32, packed, recv, s1, s2, se, sobs, slope1, slope2, slope_edge, csend, hcol,
+    bsc, qsc, inn, inn_recv, hist, ybuf, xbuf, ubuf, brow, bcol, rrow, rcol,
     fsend, frecv, bsend, brecv, psend, precv, isend, irecv, loaded,
 ):
     chan, height = x_ref.shape[0], x_ref.shape[1]
@@ -96,12 +96,27 @@
     def spot(r):
         return 2 * (r + 2)
 
+    even = lax.rem(lane, 2) == 0
+    edge = jnp.logical_or(first_lane, last_lane)
+    slot_of = (lane + 1) // 2
+
+    def joined(value):
+        return jnp.where(even, value, rolled(value, -LANES // 2 - 1))
+
+    def apart(value):
+        return jnp.where(lane < LANES // 2, value, rolled(value, LANES // 2 + 1))
+
+    def gathered(total, r, row):
+        return jnp.where(slot_of == r + 2, rolled(row, spot(r)), total)
+
     pair_of = lane // 2
     to_left = jnp.zeros((CP, LANES), F32)
     to_right = jnp.zeros((CP, LANES), F32)
     for r in range(height):
         row = x32[pl.ds(r, CP, stride=height), :]
         s1[pl.ds(CP, CP), block(2, r)] = row.astype(BF16)
+        s1[pl.ds(0, CP), block(2, r)] = rolled(row, 1).astype(BF16)
+        s1[pl.ds(2 * CP, CP), block(2, r)] = rolled(row, -1).astype(BF16)
         to_left = jnp.where(pair_of == r + 2, rolled(row, spot(r)), to_left)
         to_right = jnp.where(pair_of == r + 2, rolled(row, spot(r) + 2), to_right)
     csend[0] = to_left.astype(BF16)
@@ -134,16 +149,6 @@
             device_id=ids[d], device_id_type=MESH,
         )
         guarded(d)(copy.wait_send)
-
-    def column_blocks(rows, first_of, last_of):
-        to_left = jnp.zeros((CP, LANES), F32)
-        to_right = jnp.zeros((CP, LANES), F32)
-        for r in range(rows):
-            to_left = jnp.where(lane == r, pltpu.roll(first_of(r), r, 1) if r else first_of(r), to_left)
-            to_right = jnp.where(lane == r, pltpu.roll(last_of(r), r + 1, 1), to_right)
-        return to_left.astype(BF16), to_right.astype(BF16)
-
-    diag_slots = {UL: 0, UR: 1, DL: 2, DR: 3}
 
     def pair(r):
         return s1.at[pl.ds(CP, CP), block(2, r, 2)]
@@ -172,13 +177,20 @@
                 for slot in slots:
                     hcol[slot] = jnp.zeros((CP, LANES), BF16)
 
-    def shift_rows(s, rim, rows, low, low_lane, high, high_lane):
-        for r in rows:
-            row = s[pl.ds(CP, CP), block(rim, r)].astype(F32)
-            lower = jnp.where(first_lane, rolled(low, -low_lane(r)), rolled(row, 1))
-            upper = jnp.where(last_lane, rolled(high, LANES - 1 - high_lane(r)), rolled(row, -1))
-            s[pl.ds(0, CP), block(rim, r)] = lower.astype(BF16)
-            s[pl.ds(2 * CP, CP), block(rim, r)] = upper.astype(BF16)
+    def shift_far_rows():
+        for r in (-2, -1, height, height + 1):
+            row = s1[pl.ds(CP, CP), block(2, r)].astype(F32)
+            s1[pl.ds(0, CP), block(2, r)] = rolled(row, 1).astype(BF16)
+            s1[pl.ds(2 * CP, CP), block(2, r)] = rolled(row, -1).astype(BF16)
+
+    def merge_columns(at_edge, beside):
+        at_edge, beside = joined(at_edge), joined(beside)
+        for r in range(-1, height + 1):
+            row = jnp.where(edge, rolled(at_edge, -spot(r)), s2[pl.ds(CP, CP), block(1, r)].astype(F32))
+            outer = rolled(beside, -spot(r))
+            s2[pl.ds(0, CP), block(1, r)] = jnp.where(first_lane, outer, rolled(row, 1)).astype(BF16)
+            s2[pl.ds(CP, CP), block(1, r)] = row.astype(BF16)
+            s2[pl.ds(2 * CP, CP), block(1, r)] = jnp.where(last_lane, outer, rolled(row, -1)).astype(BF16)
 
     def with_corners(side, above, below):
         middle = jnp.logical_and(pair_of >= 2, pair_of < height + 2)
@@ -190,21 +202,22 @@
         low = with_corners(from_left, ul, dl)
         high = with_corners(from_right, ur, dr)
         first = csend[0].astype(F32)
-        last = rolled(csend[1].astype(F32), -1)
+        last = csend[1].astype(F32)
         for r in (-2, -1, height, height + 1):
             row = s1[pl.ds(CP, CP), block(2, r)].astype(F32)
-            first = jnp.where(lane == spot(r), rolled(row, spot(r)), first)
-            last = jnp.where(lane == spot(r), rolled(row, spot(r) + 1), last)
+            first = jnp.where(pair_of == r + 2, rolled(row, spot(r)), first)
+            last = jnp.where(pair_of == r + 2, rolled(row, spot(r) + 2), last)
         on_left = lane < LANES // 2
-        taps = (
-            jnp.where(on_left, low, rolled(last, LANES // 2)),
-            jnp.where(on_left, rolled(low, -1), rolled(high, LANES // 2)),
-            jnp.where(on_left, first, rolled(high, LANES // 2 - 1)),
-        )
+        lefts = (low, rolled(low, -1), first, rolled(first, -1))
+        rights = tuple(rolled(v, LANES // 2 - k) for v in (last, high) for k in (0, 1))
+        beside = tuple(jnp.where(on_left, lefts[j], rights[j + 1]) for j in range(3))
+        at_edge = tuple(jnp.where(on_left, lefts[j + 1], rights[j]) for j in range(3))
         for i in range(3):
             for j in range(3):
-                se[i, pl.ds(j * CP, CP), :] = rolled(taps[j], 2 * (1 - i)).astype(BF16)
-        return low, high, taps[1]
+                part = pl.ds(j * CP, CP)
+                se[i, part, pl.ds(0, LANES)] = rolled(beside[j], 2 * (1 - i)).astype(BF16)
+                se[i, part, pl.ds(LANES, LANES)] = rolled(at_edge[j], 2 * (1 - i)).astype(BF16)
+        return jnp.concatenate([beside[1], at_edge[1]], axis=1)
 
     def network(window, centre):
         pre = sum(dot(wt_ref[i], window(i)) for i in range(3))
@@ -212,11 +225,11 @@
         update = dot(wo_ref[...], (pre * cdf).astype(BF16))
         return centre.astype(F32) + update, lambda: cdf + pre * jnp.exp(-0.5 * pre * pre) * NORM_DENSITY
 
-    def forward_chunk(s, rim, n, slope):
+    def forward_chunk(s, rim, n, slope, inner_only):
         state, tangent = network(
             lambda i: s[:, block(rim, 2 * n + i - 1, 2)], s[pl.ds(CP, CP), block(rim, 2 * n, 2)]
         )
-        slope[:, pl.ds(n * WIDE, WIDE)] = tangent()
+        slope[:, pl.ds(n * WIDE, WIDE)] = jnp.where(edge_wide, 0.0, tangent()) if inner_only else tangent()
         return state.astype(BF16)
 
     def first_rim(centre):
@@ -228,10 +241,13 @@
         )
         s2[pl.ds(CP, CP), block(1, -1)] = (state[:, :LANES] * up).astype(BF16)
         s2[pl.ds(CP, CP), block(1, height)] = (state[:, LANES:] * down).astype(BF16)
-        sides, _ = network(lambda i: se[i], centre)
+        sides, tangent = network(lambda i: se[i], centre)
         place = lax.rem(lane, LANES // 2)
         inside = jnp.where(place == spot(-1), up, jnp.where(place == spot(height), down, 1.0))
-        return (sides * inside).astype(BF16).astype(F32)
+        here = lax.rem(lane_iota(hid), LANES // 2)
+        kept = jnp.logical_and(lax.rem(here, 2) == 0, jnp.logical_and(here >= spot(0), here <= spot(height - 1)))
+        slope_edge[...] = jnp.where(kept, tangent()[:, LANES:], 0.0)
+        return tuple((sides[:, k * LANES : (k + 1) * LANES] * inside).astype(BF16).astype(F32) for k in (0, 1))
 
     pl.semaphore_wait(barrier, owners - 1)
     send_state()
@@ -285,18 +301,27 @@
     s1[pl.ds(3 * CP, hid - 3 * CP), :] = ones((height + 4) * LANES)
     s2[pl.ds(3 * CP, hid - 3 * CP), :] = ones((height + 2) * LANES)
     for i in range(3):
-        se[i, pl.ds(3 * CP, hid - 3 * CP), :] = ones(LANES)
-
+        se[i, pl.ds(3 * CP, hid - 3 * CP), :] = ones(WIDE)
+
+    column_wide = lax.broadcasted_iota(jnp.int32, (hid, WIDE), 1)
+    column_wide = lax.rem(column_wide, LANES)
+    edge_wide = jnp.logical_or(column_wide == 0, column_wide == LANES - 1)
+    early = range(1, chunks - 1)
+
+    def first_step(n):
+        s2[pl.ds(CP, CP), block(1, 2 * n, 2)] = forward_chunk(s1, 2, n, slope1, True)
+
+    for k, n in enumerate(early):
+        to_some(k, len(early), post)
+        first_step(n)
     receive_state()
-    low, high, beside = spread_columns()
-    shift_rows(s1, 2, range(-2, height + 2), low, lambda r: spot(r) + 1, high, spot)
+    shift_far_rows()
+    first_step(0)
+    first_step(chunks - 1)
+    beside, at_edge = first_rim(spread_columns())
+    merge_columns(at_edge, beside)
     for n in range(chunks):
-        to_some(n, chunks, post)
-        s2[pl.ds(CP, CP), block(1, 2 * n, 2)] = forward_chunk(s1, 2, n, slope1)
-    sides = first_rim(beside)
-    shift_rows(s2, 1, range(-1, height + 1), sides, spot, sides, lambda r: LANES // 2 + spot(r))
-    for n in range(chunks):
-        sobs[n] = forward_chunk(s2, 1, n, slope2)
+        sobs[n] = forward_chunk(s2, 1, n, slope2, False)
 
     others = pl.ds(0, (owners - 1) * 8)
     pltpu.make_async_remote_copy(
@@ -365,84 +390,146 @@
         return total
 
     def rim_sources(t):
-        return {
-            UP: brow.at[t, 0], UL: brow.at[t, 1], UR: brow.at[t, 2],
-            DOWN: brow.at[t, 3], DL: brow.at[t, 4], DR: brow.at[t, 5],
-            LEFT: bcol.at[t, 0], RIGHT: bcol.at[t, 1],
-        }
+        table = dict.fromkeys((LEFT, RIGHT, UL, UR, DL, DR), bcol.at[t])
+        return table | {UP: brow.at[t, 0], DOWN: brow.at[t, 1]}
 
     def rim_targets(t):
-        table = {UP: rrow.at[t, 0], DOWN: rrow.at[t, 1], LEFT: rcol.at[t, 0], RIGHT: rcol.at[t, 1]}
-        for d, slot in diag_slots.items():
-            table[d] = rdiag.at[t, slot]
-        return table
-
-    pad = jnp.zeros((LANES - CP, WIDE), BF16)
-
-    def backward_step(t, cotangent, slope, finish):
+        table = {d: rcol.at[t, k] for k, d in enumerate((LEFT, RIGHT, UL, UR, DL, DR))}
+        return table | {UP: rrow.at[t, 0], DOWN: rrow.at[t, 1]}
+
+    def spread_of(cotangent, slope):
+        breadth = cotangent.shape[1]
+        rounded = jnp.concatenate([cotangent.astype(BF16), jnp.zeros((LANES - CP, breadth), BF16)], axis=0)
+        return (dot(wot_ref[...], rounded) * slope).astype(BF16)
+
+    def products(cotangent, slope):
+        for n in range(chunks):
+            cells = pl.ds(n * WIDE, WIDE)
+            spread = spread_of(cotangent(n), slope[:, cells])
+            for i in range(3):
+                ybuf[pl.ds(3 * i * CP, 3 * CP), cells] = dot(wk[i, pl.ds(0, 3 * CP), :], spread)
+
+    def inner(t_low, t_mid, t_high):
+        return (
+            t_mid
+            + jnp.where(first_lane, 0.0, rolled(t_high, 1))
+            + jnp.where(last_lane, 0.0, rolled(t_low, -1))
+        )
+
+    def local_sums(t, own):
+        columns = jnp.zeros((CP, LANES), F32)
+        for r in range(-1, height + 1):
+            t_low, t_mid, t_high = (summed(j, r) for j in (-1, 0, 1))
+            total = inner(t_low, t_mid, t_high)
+            ubuf[t, :, block(1, r)] = total + own(r) if 0 <= r < height and own else total
+            columns = gathered(columns, r, jnp.where(first_lane, t_low, t_high))
+        return columns
+
+    def send_rim(t, above, below, columns):
+        brow[t, 0] = above.astype(BF16)
+        brow[t, 1] = below.astype(BF16)
+        bcol[t] = columns.astype(BF16)
         src, dst = rim_sources(t), rim_targets(t)
-        for n in range(chunks):
-            rounded = jnp.concatenate([cotangent(n).astype(BF16), pad], axis=0)
-            spread = (dot(wot_ref[...], rounded) * slope[:, pl.ds(n * WIDE, WIDE)]).astype(BF16)
-            for i in range(3):
-                ybuf[pl.ds(3 * i * CP, 3 * CP), pl.ds(n * WIDE, WIDE)] = dot(wk[i, pl.ds(0, 3 * CP), :], spread)
-
-        def inner(t_low, t_mid, t_high):
-            return (
-                t_mid
-                + jnp.where(first_lane, 0.0, pltpu.roll(t_high, 1, 1))
-                + jnp.where(last_lane, 0.0, pltpu.roll(t_low, LANES - 1, 1))
-            )
-
-        for r, at in ((-1, 0), (height, 3)):
-            t_low, t_mid, t_high = (summed(j, r) for j in (-1, 0, 1))
-            brow[t, at] = inner(t_low, t_mid, t_high).astype(BF16)
-            brow[t, at + 1] = t_low.astype(BF16)
-            brow[t, at + 2] = t_high.astype(BF16)
-        for d in (UP, DOWN, UL, UR, DL, DR):
+        for d in (UP, DOWN, LEFT, RIGHT, UL, UR, DL, DR):
             send(src[d], dst[opposite[d]], t, d, bsend, brecv)
-        to_left, to_right = column_blocks(height, lambda r: summed(-1, r), lambda r: summed(1, r))
-        bcol[t, 0] = to_left
-        bcol[t, 1] = to_right
-        for d in (LEFT, RIGHT):
-            send(src[d], dst[opposite[d]], t, d, bsend, brecv)
-        for r in range(height):
-            to_some(height * t + r, 2 * height, give_back)
-            ubuf[:, pl.ds(r * LANES, LANES)] = inner(summed(-1, r), summed(0, r), summed(1, r)) + cotangent(r // 2)[
-                :, (r % 2) * LANES : (r % 2 + 1) * LANES
-            ]
+
+    def receive_rim(t):
+        dst = rim_targets(t)
         for d in range(8):
             wait_recv(dst[d], t, d, bsend, brecv)
-        for r, there, at, a, b in ((0, has_up, 0, UL, UR), (height - 1, has_down, 1, DL, DR)):
-
-            @pl.when(there)
+        for there, row, slots in ((has_up, 0, (2, 3)), (has_down, 1, (4, 5))):
+
+            @pl.when(jnp.logical_not(there))
             def _():
-                ubuf[:, pl.ds(r * LANES, LANES)] = (
-                    ubuf[:, pl.ds(r * LANES, LANES)]
-                    + rrow[t, at].astype(F32)
-                    + jnp.where(first_lane, pltpu.roll(rdiag[t, diag_slots[a]].astype(F32), 1, 1), 0.0)
-                    + jnp.where(last_lane, pltpu.roll(rdiag[t, diag_slots[b]].astype(F32), LANES - 1, 1), 0.0)
-                )
-
-        from_left = rcol[t, 0].astype(F32)
-        from_right = rcol[t, 1].astype(F32)
-        for r in range(height):
-            finish(
-                r,
-                ubuf[:, pl.ds(r * LANES, LANES)]
-                + jnp.where(first_lane, pltpu.roll(from_left, (LANES - r) % LANES, 1) if r else from_left, 0.0)
-                + jnp.where(last_lane, pltpu.roll(from_right, LANES - 1 - r, 1), 0.0),
+                rrow[t, row] = jnp.zeros((CP, LANES), BF16)
+                for slot in slots:
+                    rcol[t, slot] = jnp.zeros((CP, LANES), BF16)
+
+        from_left, from_right, ul, ur, dl, dr = (rcol[t, k].astype(F32) for k in range(6))
+        inside = jnp.logical_and(slot_of >= 2, slot_of < height + 2)
+        inflow = jnp.where(inside, jnp.where(even, rolled(from_left, 1), rolled(from_right, -1)), 0.0)
+        top, bottom, past, before = spot(0), spot(height - 1), spot(height), spot(-1)
+        for value, came, goes in (
+            (ul, past - 1, top), (ur, past, top - 1), (dl, before - 1, bottom), (dr, before, bottom - 1),
+        ):
+            inflow = inflow + jnp.where(lane == goes, rolled(value, goes - came), 0.0)
+        return rrow[t, 0].astype(F32), rrow[t, 1].astype(F32), inflow
+
+    products(lambda n: hist[last[n]], slope2)
+    columns = local_sums(0, lambda r: hist[last[r // 2]][:, (r % 2) * LANES : (r % 2 + 1) * LANES])
+    send_rim(0, ubuf[0, :, block(1, -1)], ubuf[0, :, block(1, height)], columns)
+
+    to_some(0, 2, give_back)
+    products(lambda n: ubuf[0, :, block(1, 2 * n, 2)], slope1)
+    columns = local_sums(1, None)
+    at_edge = jnp.zeros((CP, LANES), F32)
+    for r in range(height):
+        at_edge = gathered(at_edge, r, ubuf[0, :, block(1, r)])
+    to_some(1, 2, give_back)
+    above, below, inflow = receive_rim(0)
+    far = height - 1
+    at_edge = at_edge + inflow
+    at_edge = at_edge + gathered(gathered(jnp.zeros((CP, LANES), F32), 0, above), far, below)
+    late = spread_of(
+        jnp.concatenate([above, below, apart(at_edge)], axis=1),
+        jnp.concatenate(
+            [slope1[:, pl.ds(0, LANES)], slope1[:, pl.ds(far * LANES, LANES)], slope_edge[...]], axis=1
+        ),
+    )
+    for i in range(3):
+        xbuf[pl.ds(3 * i * CP, 3 * CP), :] = dot(wk[i, pl.ds(0, 3 * CP), :], late)
+
+    def late_tap(i, j, part):
+        return xbuf[pl.ds((3 * (i + 1) + j + 1) * CP, CP), pl.ds(part * LANES, LANES)]
+
+    def late_row(part, i):
+        return tuple(late_tap(i, j, part) for j in (-1, 0, 1))
+
+    to_low, to_same, to_high = (
+        sum(rolled(late_tap(i, j, 2), 2 * i) for i in (-1, 0, 1)) for j in (-1, 0, 1)
+    )
+    outside = slot_of <= height + 2
+    columns = columns + jnp.where(outside, jnp.where(even, to_low, rolled(to_high, -LANES // 2 - 1)), 0.0)
+    for part, base in ((0, 0), (1, far)):
+        for i in (-1, 0, 1):
+            t_low, _, t_high = late_row(part, i)
+            columns = columns + gathered(
+                jnp.zeros((CP, LANES), F32), base + i, jnp.where(first_lane, t_low, t_high)
             )
-
-    def keep(r, value):
-        gbuf[:, pl.ds(r * LANES, LANES)] = value
-
-    def write(r, value):
+    same = joined(to_same)
+    next_in = jnp.where(even, rolled(to_low, -LANES // 2 - 2), rolled(to_high, 1))
+    second = jnp.logical_or(lane == 1, lane == LANES - 2)
+
+    def from_columns(r, outermost):
+        return jnp.where(edge, rolled(outermost, -spot(r)), 0.0) + jnp.where(second, rolled(next_in, -spot(r)), 0.0)
+
+    send_rim(
+        1,
+        ubuf[1, :, block(1, -1)] + inner(*late_row(0, -1)) + from_columns(-1, same),
+        ubuf[1, :, block(1, height)] + inner(*late_row(1, 1)) + from_columns(height, same),
+        columns,
+    )
+    outermost = same + inflow
+    for r in range(height):
+        value = ubuf[0, :, block(1, r)] + ubuf[1, :, block(1, r)] + from_columns(r, outermost)
+        if r < 2:
+            value = value + inner(*late_row(0, r))
+        if r >= far - 1:
+            value = value + inner(*late_row(1, r - far))
+        if r == 0:
+            value = value + above
+        if r == far:
+            value = value + below
+        ubuf[0, :, block(1, r)] = value
+    above, below, inflow = receive_rim(1)
+    for r in range(height):
+        value = ubuf[0, :, block(1, r)] + jnp.where(edge, rolled(inflow, -spot(r)), 0.0)
+        if r == 0:
+            value = value + above
+        if r == far:
+            value = value + below
         here = pl.ds(r, chan, stride=height)
         grad_ref[here, :] = grad_ref[here, :] + value[:chan]
-
-    backward_step(0, lambda n: hist[last[n]], slope2, keep)
-    backward_step(1, lambda n: gbuf[:, pl.ds(n * WIDE, WIDE)], slope1, write)
 
     rows = pl.ds(0, owners - 1)
     pltpu.make_async_remote_copy(
@@ -514,10 +601,11 @@
             pltpu.VMEM((owners * 8, LANES), F32),
             pltpu.VMEM((hid, (height + 4) * LANES), BF16),
             pltpu.VMEM((hid, (height + 2) * LANES), BF16),
-            pltpu.VMEM((3, hid, LANES), BF16),
+            pltpu.VMEM((3, hid, WIDE), BF16),
             pltpu.VMEM((chunks, CP, WIDE), BF16),
             pltpu.VMEM((hid, cells), F32),
             pltpu.VMEM((hid, cells), F32),
+            pltpu.VMEM((hid, LANES), F32),
             pltpu.VMEM((2, CP, LANES), BF16),
             pltpu.VMEM((6, CP, LANES), BF16),
             pltpu.VMEM((owners, WIDE, LANES), BF16),
@@ -526,13 +614,12 @@
             pltpu.VMEM((owners, 1, LANES), F32),
             pltpu.VMEM((owners + 1, CP, WIDE), F32),
             pltpu.VMEM((9 * CP, cells), F32),
-            pltpu.VMEM((CP, cells), F32),
-            pltpu.VMEM((CP, cells), F32),
+            pltpu.VMEM((9 * CP, 3 * LANES), F32),
+            pltpu.VMEM((2, CP, (height + 2) * LANES), F32),
+            pltpu.VMEM((2, 2, CP, LANES), BF16),
+            pltpu.VMEM((2, CP, LANES), BF16),
+            pltpu.VMEM((2, 2, CP, LANES), BF16),
             pltpu.VMEM((2, 6, CP, LANES), BF16),
-            pltpu.VMEM((2, 2, CP, LANES), BF16),
-            pltpu.VMEM((2, 2, CP, LANES), BF16),
-            pltpu.VMEM((2, 4, CP, LANES), BF16),
-            pltpu.VMEM((2, 2, CP, LANES), BF16),
             dma((1, 8)), dma((1, 8)), dma((2, 8)), dma((2, 8)),
             dma, dma, dma, dma, dma((6,)),
         ],

time: 56.4 us -> 53.6 us (0.950)
  Pallas kernels: 55.4 us -> 52.6 us
    pallas_call x1, Pallas kernels: 53.5 us -> 50.8 us  [local(): pl.pallas_call(functools.partial(kernel, n_lat, n_lon, hid), out_shape=(j...]
where the time goes in v4:
time: 53.6 us; the launch traced here: 53.4 us
  Pallas kernels  52.6 us (98%)
  between operations  0.8 us (1%)
    pallas_call x1, Pallas kernels, local(): pl.pallas_call(functools.partial(kernel, n_lat, n_lon, hid), out_shape=(j...  50.8 us
    pallas_call x1, Pallas kernels, local(): pl.pallas_call(hand_over, out_shape=(jax.ShapeDtypeStruct((chan, height,...  1.87 us

profile of v4, /device:TPU:1, one launch (start us, length us, event | category | flops | bytes accessed | tf_op | source)
XLA Modules:
  0.0 53.4 jit_solution(13653274811657943902)
XLA Ops:
  0.6 50.8 %shard_map.122 = (f32[1104,128]{1,0:T(8,128)}, f32[128,128]{1,0:T(8,128)}) custom-call(bf16[69,16,128]{2,1,0:T(8,128)(2,1)} %x_hbm.1, bf16[69,16,128]{2,1,0:T(8,128)(2,1)} %xb_hbm.1, f32[1,69]{1,0:T(1,128)} %bitcast.15, bf16[9,69,256]{2,1,0:T(8,128)(2,1)} %cw_ref.1, f32[1,256]{1,0:T(1,128)} %bitcast.14, bf16[69,256]{1,0:T(8,128)(2,1)} %ow_ref.1, ...), custom_call_target="tpu_custom_call" | custom-call | tf_op jit(solution)/shard_map/pallas_call | solution.py:579
  51.4 1.9 %shard_map.123 = (f32[69,16,128]{2,1,0:T(8,128)}, f32[1,128,128]{2,1,0:T(8,128)}) custom-call(f32[69,16,128]{2,1,0:T(8,128)} %bitcast.8, f32[1,128,128]{2,1,0:T(8,128)} %bitcast.13), custom_call_target="tpu_custom_call" | custom-call | tf_op jit(solution)/shard_map/pallas_call | solution.py:633

commit v5 on v4

--- a/solution.py
+++ b/solution.py
@@ -16,8 +16,14 @@
 ROOT_HALF = 0.7071067811865476
 NORM_DENSITY = 0.3989422804014327
 UP, DOWN, LEFT, RIGHT, UL, UR, DL, DR = range(8)
-GROUP = 16
+GROUP = 32
+LAG = 3
 PIECES = 3
+WORD = 65536
+HALF_WORD = 32768
+HALF_WORDS = 65535.0
+TOP_PRECISION = 3.0
+VALUE_STEPS = 2.0**28
 
 
 def dot(a, b):
@@ -32,7 +38,7 @@
     n_lat, n_lon, hid,
     x_hbm, xb_hbm, bp_ref, cw_ref, cb_ref, ow_ref, swath_ref, cell_hbm, w_hbm, val_hbm, prec_hbm,
     grad_ref, innov_ref,
-    x_ref, xb_ref, cell_ref, w_ref, val_ref, prec_ref, wpad, wk, wt_ref, wo_ref, wot_ref, x32, packed, recv, s1, s2, se, sobs, slope1, slope2, slope_edge, csend, hcol,
+    x_ref, xb_ref, cell_ref, w_ref, val_ref, prec_ref, wpad, wk, wt_ref, wo_ref, wot_ref, x32, packed, recv, opened, s1, s2, se, sobs, slope1, slope2, slope_edge, csend, hcol,
     bsc, qsc, inn, inn_recv, hist, ybuf, xbuf, ubuf, brow, bcol, rrow, rcol,
     fsend, frecv, bsend, brecv, psend, precv, isend, irecv, loaded,
 ):
@@ -219,29 +225,40 @@
                 se[i, part, pl.ds(LANES, LANES)] = rolled(at_edge[j], 2 * (1 - i)).astype(BF16)
         return jnp.concatenate([beside[1], at_edge[1]], axis=1)
 
-    def network(window, centre):
-        pre = sum(dot(wt_ref[i], window(i)) for i in range(3))
+    def conv(window):
+        return sum(dot(wt_ref[i], window(i)) for i in range(3))
+
+    def network(pre, centre):
         cdf = 0.5 * (1.0 + lax.erf(pre * ROOT_HALF))
         update = dot(wo_ref[...], (pre * cdf).astype(BF16))
         return centre.astype(F32) + update, lambda: cdf + pre * jnp.exp(-0.5 * pre * pre) * NORM_DENSITY
 
-    def forward_chunk(s, rim, n, slope, inner_only):
-        state, tangent = network(
-            lambda i: s[:, block(rim, 2 * n + i - 1, 2)], s[pl.ds(CP, CP), block(rim, 2 * n, 2)]
-        )
+    def conv_chunk(s, rim, n):
+        return conv(lambda i: s[:, block(rim, 2 * n + i - 1, 2)])
+
+    def forward_chunk(pre, s, rim, n, slope, inner_only):
+        state, tangent = network(pre, s[pl.ds(CP, CP), block(rim, 2 * n, 2)])
         slope[:, pl.ds(n * WIDE, WIDE)] = jnp.where(edge_wide, 0.0, tangent()) if inner_only else tangent()
         return state.astype(BF16)
+
+    def pipelined(order, start, finish, lag=1):
+        order = list(order)
+        held = [start(n) for n in order[:lag]]
+        for k, n in enumerate(order):
+            if k + lag < len(order):
+                held.append(start(order[k + lag]))
+            finish(n, held.pop(0))
 
     def first_rim(centre):
         up, down = has_up.astype(F32), has_down.astype(F32)
         rows = (-1, height)
         state, _ = network(
-            lambda i: jnp.concatenate([s1[:, block(2, r + i - 1)] for r in rows], axis=1),
+            conv(lambda i: jnp.concatenate([s1[:, block(2, r + i - 1)] for r in rows], axis=1)),
             jnp.concatenate([s1[pl.ds(CP, CP), block(2, r)] for r in rows], axis=1),
         )
         s2[pl.ds(CP, CP), block(1, -1)] = (state[:, :LANES] * up).astype(BF16)
         s2[pl.ds(CP, CP), block(1, height)] = (state[:, LANES:] * down).astype(BF16)
-        sides, tangent = network(lambda i: se[i], centre)
+        sides, tangent = network(conv(lambda i: se[i]), centre)
         place = lax.rem(lane, LANES // 2)
         inside = jnp.where(place == spot(-1), up, jnp.where(place == spot(height), down, 1.0))
         here = lax.rem(lane_iota(hid), LANES // 2)
@@ -254,23 +271,21 @@
 
     for load in loads[1:]:
         load.wait()
-    cell = cell_ref[...]
-    packed[pl.ds(0, owners, stride=8), :] = (cell // WIDE).astype(F32)
-    packed[pl.ds(1, owners, stride=8), :] = (cell % LANES).astype(F32)
-    for k in range(4):
-        packed[pl.ds(2 + k, owners, stride=8), :] = w_ref[k]
-    packed[pl.ds(6, owners, stride=8), :] = val_ref[...]
-    packed[pl.ds(7, owners, stride=8), :] = prec_ref[...]
+    def fixed(value, top):
+        return jnp.round(value * (HALF_WORDS / top)).astype(jnp.int32)
+
+    packed[:, 0, :] = (fixed(w_ref[0], 1.0) - HALF_WORD) * WORD + fixed(w_ref[1], 1.0)
+    packed[:, 1, :] = (fixed(w_ref[2], 1.0) - HALF_WORD) * WORD + fixed(w_ref[3], 1.0)
+    packed[:, 2, :] = cell_ref[...] * WORD + fixed(prec_ref[...], TOP_PRECISION)
+    packed[:, 3, :] = jnp.round(val_ref[...] * VALUE_STEPS).astype(jnp.int32)
 
     def post(other, where):
         pltpu.make_async_remote_copy(
-            src_ref=packed.at[pl.ds(pl.multiple_of(other * 8, 8), 8)],
-            dst_ref=recv.at[pl.ds(pl.multiple_of(me * 8, 8), 8)],
+            src_ref=packed.at[other], dst_ref=recv.at[me],
             send_sem=psend, recv_sem=precv, device_id=where, device_id_type=MESH,
         ).start()
 
-    mine = pl.ds(pl.multiple_of(me * 8, 8), 8)
-    recv[mine, :] = packed[mine, :]
+    recv[me] = packed[me]
 
     wpad[...] = jnp.zeros((LANES, hid), F32)
     bias = cb_ref[...]
@@ -308,34 +323,58 @@
     edge_wide = jnp.logical_or(column_wide == 0, column_wide == LANES - 1)
     early = range(1, chunks - 1)
 
-    def first_step(n):
-        s2[pl.ds(CP, CP), block(1, 2 * n, 2)] = forward_chunk(s1, 2, n, slope1, True)
-
-    for k, n in enumerate(early):
-        to_some(k, len(early), post)
-        first_step(n)
+    def first_conv(n):
+        return conv_chunk(s1, 2, n)
+
+    def first_step(n, pre):
+        s2[pl.ds(CP, CP), block(1, 2 * n, 2)] = forward_chunk(pre, s1, 2, n, slope1, True)
+
+    def early_step(n, pre):
+        to_some(n - 1, len(early), post)
+        first_step(n, pre)
+
+    pipelined(early, first_conv, early_step)
     receive_state()
     shift_far_rows()
-    first_step(0)
-    first_step(chunks - 1)
+    pipelined((0, chunks - 1), first_conv, first_step)
     beside, at_edge = first_rim(spread_columns())
     merge_columns(at_edge, beside)
-    for n in range(chunks):
-        sobs[n] = forward_chunk(s2, 1, n, slope2, False)
-
-    others = pl.ds(0, (owners - 1) * 8)
+
+    def second_step(n, pre):
+        sobs[n] = forward_chunk(pre, s2, 1, n, slope2, False)
+
+    pipelined(range(chunks), lambda n: conv_chunk(s2, 1, n), second_step)
+
+    others = pl.ds(0, owners - 1)
     pltpu.make_async_remote_copy(
         src_ref=packed.at[others], dst_ref=recv.at[others], send_sem=psend, recv_sem=precv,
         device_id=ids[RIGHT], device_id_type=MESH,
     ).wait()
+
+    def unfixed(value, top):
+        return value.astype(F32) * (top / HALF_WORDS)
+
+    def field(k, value):
+        opened[pl.ds(k, owners, stride=8), :] = value
+
+    words = recv[:, 2, :]
+    field(0, (words >> 24).astype(F32))
+    field(1, ((words >> 16) & (LANES - 1)).astype(F32))
+    field(7, unfixed(words & (WORD - 1), TOP_PRECISION))
+    for k in range(2):
+        words = recv[:, k, :]
+        field(2 + 2 * k, unfixed((words >> 16) + HALF_WORD, 1.0))
+        field(3 + 2 * k, unfixed(words & (WORD - 1), 1.0))
+    field(6, recv[:, 3, :].astype(F32) * (1.0 / VALUE_STEPS))
     column = lax.broadcasted_iota(jnp.int32, (LANES, LANES), 0).astype(F32).astype(BF16)
     channel = lax.broadcasted_iota(jnp.int32, (CP, LANES), 0).astype(F32)
     zero = jnp.zeros((LANES, LANES), BF16)
 
     def estimate(group, carry):
-        for u in range(GROUP):
+        def start(u):
             k = group * GROUP + u
-            packet = recv[pl.ds(pl.multiple_of(k * 8, 8), 8), :]
+            packet = opened[pl.ds(pl.multiple_of(k * 8, 8), 8), :]
+
             def row(which):
                 return jnp.broadcast_to(packet[which : which + 1].astype(BF16), (LANES, LANES))
 
@@ -349,25 +388,38 @@
                 axis=0,
             )
             bsc[k] = table
+            return packet, dot(sobs[swath_ref[0, k]], table)
+
+        def finish(u, given):
+            k = group * GROUP + u
+            packet, found = given
             picked = channel == packet[0:1]
-            found = dot(sobs[swath_ref[0, k]], table)
             gap = jnp.sum(jnp.where(picked, found, 0.0), axis=0, keepdims=True) - packet[6:7]
             inn[k] = gap
             qsc[k] = jnp.where(picked, packet[7:8] * gap, 0.0).astype(BF16)
+
+        pipelined(range(GROUP), start, finish, LAG)
         return carry
 
     lax.fori_loop(0, owners // GROUP, estimate, 0)
     hist[0] = jnp.zeros((CP, WIDE), F32)
 
     def pull(group, last):
-        for u in range(GROUP):
+        slots = [last]
+
+        def start(u):
+            k = group * GROUP + u
+            return lax.dot_general(qsc[k], bsc[k], (((1,), (1,)), ((), ())), preferred_element_type=F32)
+
+        def finish(u, share):
             k = group * GROUP + u
             patch = swath_ref[0, k]
-            before = sum(jnp.where(patch == m, last[m], 0) for m in range(chunks))
-            share = lax.dot_general(qsc[k], bsc[k], (((1,), (1,)), ((), ())), preferred_element_type=F32)
+            before = sum(jnp.where(patch == m, slots[-1][m], 0) for m in range(chunks))
             hist[k + 1] = hist[before] + share
-            last = tuple(jnp.where(patch == m, k + 1, last[m]) for m in range(chunks))
-        return last
+            slots.append(tuple(jnp.where(patch == m, k + 1, slots[-1][m]) for m in range(chunks)))
+
+        pipelined(range(GROUP), start, finish, LAG)
+        return slots[-1]
 
     last = lax.fori_loop(0, owners // GROUP, pull, (jnp.int32(0),) * chunks)
     inn_recv[me] = inn[me]
@@ -403,11 +455,14 @@
         return (dot(wot_ref[...], rounded) * slope).astype(BF16)
 
     def products(cotangent, slope):
-        for n in range(chunks):
-            cells = pl.ds(n * WIDE, WIDE)
-            spread = spread_of(cotangent(n), slope[:, cells])
+        def start(n):
+            return spread_of(cotangent(n), slope[:, pl.ds(n * WIDE, WIDE)])
+
+        def finish(n, spread):
             for i in range(3):
-                ybuf[pl.ds(3 * i * CP, 3 * CP), cells] = dot(wk[i, pl.ds(0, 3 * CP), :], spread)
+                ybuf[pl.ds(3 * i * CP, 3 * CP), pl.ds(n * WIDE, WIDE)] = dot(wk[i, pl.ds(0, 3 * CP), :], spread)
+
+        pipelined(range(chunks), start, finish)
 
     def inner(t_low, t_mid, t_high):
         return (
@@ -597,7 +652,8 @@
             pltpu.VMEM((CP, hid), BF16),
             pltpu.VMEM((hid, LANES), BF16),
             pltpu.VMEM((CP * height, LANES), F32),
-            pltpu.VMEM((owners * 8, LANES), F32),
+            pltpu.VMEM((owners, 4, LANES), jnp.int32),
+            pltpu.VMEM((owners, 4, LANES), jnp.int32),
             pltpu.VMEM((owners * 8, LANES), F32),
             pltpu.VMEM((hid, (height + 4) * LANES), BF16),
             pltpu.VMEM((hid, (height + 2) * LANES), BF16),

time: 53.6 us -> 48.4 us (0.903)
  Pallas kernels: 52.6 us -> 47.4 us
    pallas_call x1, Pallas kernels: 50.8 us -> 45.6 us  [local(): pl.pallas_call(functools.partial(kernel, n_lat, n_lon, hid), out_shape=(j...]
where the time goes in v5:
time: 48.4 us; the launch traced here: 48.2 us
  Pallas kernels  47.4 us (98%)
  between operations  0.8 us (2%)
    pallas_call x1, Pallas kernels, local(): pl.pallas_call(functools.partial(kernel, n_lat, n_lon, hid), out_shape=(j...  45.6 us
    pallas_call x1, Pallas kernels, local(): pl.pallas_call(hand_over, out_shape=(jax.ShapeDtypeStruct((chan, height,...  1.87 us

profile of v5, /device:TPU:1, one launch (start us, length us, event | category | flops | bytes accessed | tf_op | source)
XLA Modules:
  0.0 48.2 jit_solution(11295267370622601449)
XLA Ops:
  0.6 45.6 %shard_map.122 = (f32[1104,128]{1,0:T(8,128)}, f32[128,128]{1,0:T(8,128)}) custom-call(bf16[69,16,128]{2,1,0:T(8,128)(2,1)} %x_hbm.1, bf16[69,16,128]{2,1,0:T(8,128)(2,1)} %xb_hbm.1, f32[1,69]{1,0:T(1,128)} %bitcast.15, bf16[9,69,256]{2,1,0:T(8,128)(2,1)} %cw_ref.1, f32[1,256]{1,0:T(1,128)} %bitcast.14, bf16[69,256]{1,0:T(8,128)(2,1)} %ow_ref.1, ...), custom_call_target="tpu_custom_call" | custom-call | tf_op jit(solution)/shard_map/pallas_call | solution.py:634
  46.2 1.9 %shard_map.123 = (f32[69,16,128]{2,1,0:T(8,128)}, f32[1,128,128]{2,1,0:T(8,128)}) custom-call(f32[69,16,128]{2,1,0:T(8,128)} %bitcast.8, f32[1,128,128]{2,1,0:T(8,128)} %bitcast.13), custom_call_target="tpu_custom_call" | custom-call | tf_op jit(solution)/shard_map/pallas_call | solution.py:689

commit v6 on v5

--- a/solution.py
+++ b/solution.py
@@ -38,16 +38,15 @@
     n_lat, n_lon, hid,
     x_hbm, xb_hbm, bp_ref, cw_ref, cb_ref, ow_ref, swath_ref, cell_hbm, w_hbm, val_hbm, prec_hbm,
     grad_ref, innov_ref,
-    x_ref, xb_ref, cell_ref, w_ref, val_ref, prec_ref, wpad, wk, wt_ref, wo_ref, wot_ref, x32, packed, recv, opened, s1, s2, se, sobs, slope1, slope2, slope_edge, csend, hcol,
-    bsc, qsc, inn, inn_recv, hist, ybuf, xbuf, ubuf, brow, bcol, rrow, rcol,
-    fsend, frecv, bsend, brecv, psend, precv, isend, irecv, loaded,
+    x_ref, xb_ref, cell_ref, w_ref, val_ref, prec_ref, wpad, wk, wt_ref, wo_ref, wot_ref, x32, given, packed, recv, opened, s1, s2, se, sobs, slope1, slope2, slope_edge, csend, hcol,
+    bsc, qsc, inn, inn_recv, inn_mate, hist, ybuf, xbuf, ubuf, brow, bcol, rrow, rcol,
+    fsend, frecv, bsend, brecv, psend, precv, isend, irecv, gsend, grecv, loaded,
 ):
     chan, height = x_ref.shape[0], x_ref.shape[1]
     owners = n_lat * n_lon
     chunks = height // 2
     lat = lax.axis_index("lat")
     lon = lax.axis_index("lon")
-    me = lat * n_lon + lon
     has_up = lat > 0
     has_down = lat < n_lat - 1
     left = lax.rem(lon + n_lon - 1, n_lon)
@@ -63,15 +62,27 @@
     def wrapped(value, count):
         return value - jnp.where(value >= count, count, 0)
 
-    rounds = [(step, ahead) for step in range(n_lat) for ahead in range(n_lon) if step or ahead]
+    side, half = lax.rem(lat, 2), lat // 2
+    halves = n_lat // 2
+    pairs = halves * n_lon
+    mate = {"lat": lat + 1 - 2 * side}
+    my_pair = half * n_lon + lon
+    rounds = [(step, ahead) for step in range(halves) for ahead in range(n_lon) if step or ahead]
 
     def to_some(part, parts, act):
         for step, ahead in rounds[len(rounds) * part // parts : len(rounds) * (part + 1) // parts]:
-            there, column = wrapped(lat + step, n_lat), wrapped(lon + ahead, n_lon)
-            act(there * n_lon + column, (there, column))
+            there, column = wrapped(half + step, halves), wrapped(lon + ahead, n_lon)
+            act(there * n_lon + column, (2 * there + side, column))
+
+    def rows_of(which, ref):
+        return jnp.concatenate(
+            [ref[pl.ds(pl.multiple_of((2 * h + which) * n_lon, n_lon), n_lon), :] for h in range(halves)], axis=0
+        )
 
     def greet(_, where):
         pl.semaphore_signal(barrier, inc=1, device_id=where, device_id_type=MESH)
+
+    across = {UP: has_up, UL: has_up, UR: has_up, DOWN: has_down, DL: has_down, DR: has_down}
 
     loads = [
         pltpu.make_async_copy(src, dst, loaded.at[k])
@@ -85,6 +96,8 @@
     for load in loads:
         load.start()
     to_some(0, 1, greet)
+    for d, there in across.items():
+        pl.when(there)(functools.partial(greet, None, ids[d]))
 
     x32[pl.ds(chan * height, (CP - chan) * height), :] = jnp.zeros(((CP - chan) * height, LANES), F32)
     loads[0].wait()
@@ -266,7 +279,7 @@
         slope_edge[...] = jnp.where(kept, tangent()[:, LANES:], 0.0)
         return tuple((sides[:, k * LANES : (k + 1) * LANES] * inside).astype(BF16).astype(F32) for k in (0, 1))
 
-    pl.semaphore_wait(barrier, owners - 1)
+    pl.semaphore_wait(barrier, pairs - 1 + 3 * (has_up.astype(jnp.int32) + has_down.astype(jnp.int32)))
     send_state()
 
     for load in loads[1:]:
@@ -274,18 +287,30 @@
     def fixed(value, top):
         return jnp.round(value * (HALF_WORDS / top)).astype(jnp.int32)
 
-    packed[:, 0, :] = (fixed(w_ref[0], 1.0) - HALF_WORD) * WORD + fixed(w_ref[1], 1.0)
-    packed[:, 1, :] = (fixed(w_ref[2], 1.0) - HALF_WORD) * WORD + fixed(w_ref[3], 1.0)
-    packed[:, 2, :] = cell_ref[...] * WORD + fixed(prec_ref[...], TOP_PRECISION)
-    packed[:, 3, :] = jnp.round(val_ref[...] * VALUE_STEPS).astype(jnp.int32)
+    def packet_words(which):
+        first, second, third, fourth = (fixed(rows_of(which, w_ref.at[k]), 1.0) for k in range(4))
+        return (
+            (first - HALF_WORD) * WORD + second,
+            (third - HALF_WORD) * WORD + fourth,
+            rows_of(which, cell_ref) * WORD + fixed(rows_of(which, prec_ref), TOP_PRECISION),
+            jnp.round(rows_of(which, val_ref) * VALUE_STEPS).astype(jnp.int32),
+        )
+
+    for k, word in enumerate(packet_words(1 - side)):
+        given[:, k, :] = word
+    to_mate = pltpu.make_async_remote_copy(
+        src_ref=given, dst_ref=packed.at[1], send_sem=gsend.at[0], recv_sem=grecv.at[0],
+        device_id=mate, device_id_type=MESH,
+    )
+    to_mate.start()
+    for k, word in enumerate(packet_words(side)):
+        packed[0, :, k, :] = word
 
     def post(other, where):
         pltpu.make_async_remote_copy(
-            src_ref=packed.at[other], dst_ref=recv.at[me],
+            src_ref=packed.at[:, other], dst_ref=recv.at[:, my_pair],
             send_sem=psend, recv_sem=precv, device_id=where, device_id_type=MESH,
         ).start()
-
-    recv[me] = packed[me]
 
     wpad[...] = jnp.zeros((LANES, hid), F32)
     bias = cb_ref[...]
@@ -333,6 +358,8 @@
         to_some(n - 1, len(early), post)
         first_step(n, pre)
 
+    to_mate.wait_recv()
+    recv[:, my_pair] = packed[:, my_pair]
     pipelined(early, first_conv, early_step)
     receive_state()
     shift_far_rows()
@@ -345,27 +372,37 @@
 
     pipelined(range(chunks), lambda n: conv_chunk(s2, 1, n), second_step)
 
-    others = pl.ds(0, owners - 1)
+    others = pl.ds(0, pairs - 1)
     pltpu.make_async_remote_copy(
-        src_ref=packed.at[others], dst_ref=recv.at[others], send_sem=psend, recv_sem=precv,
+        src_ref=packed.at[:, others], dst_ref=recv.at[:, others], send_sem=psend, recv_sem=precv,
         device_id=ids[RIGHT], device_id_type=MESH,
     ).wait()
 
     def unfixed(value, top):
         return value.astype(F32) * (top / HALF_WORDS)
 
-    def field(k, value):
-        opened[pl.ds(k, owners, stride=8), :] = value
-
-    words = recv[:, 2, :]
-    field(0, (words >> 24).astype(F32))
-    field(1, ((words >> 16) & (LANES - 1)).astype(F32))
-    field(7, unfixed(words & (WORD - 1), TOP_PRECISION))
-    for k in range(2):
-        words = recv[:, k, :]
-        field(2 + 2 * k, unfixed((words >> 16) + HALF_WORD, 1.0))
-        field(3 + 2 * k, unfixed(words & (WORD - 1), 1.0))
-    field(6, recv[:, 3, :].astype(F32) * (1.0 / VALUE_STEPS))
+    for which in range(2):
+
+        def field(k, value, which=which):
+            opened[pl.ds(which * pairs * 8 + k, pairs, stride=8), :] = value
+
+        words = recv[which, :, 2, :]
+        field(0, (words >> 24).astype(F32))
+        field(1, ((words >> 16) & (LANES - 1)).astype(F32))
+        field(7, unfixed(words & (WORD - 1), TOP_PRECISION))
+        for k in range(2):
+            words = recv[which, :, k, :]
+            field(2 + 2 * k, unfixed((words >> 16) + HALF_WORD, 1.0))
+            field(3 + 2 * k, unfixed(words & (WORD - 1), 1.0))
+        field(6, recv[which, :, 3, :].astype(F32) * (1.0 / VALUE_STEPS))
+
+    def patch_of(group, u):
+        k = group * GROUP + u
+        which, pair_id = k // pairs, lax.rem(k, pairs)
+        at_side = jnp.where(which == 0, side, 1 - side)
+        owner = (2 * (pair_id // n_lon) + at_side) * n_lon + lax.rem(pair_id, n_lon)
+        return swath_ref[0, owner]
+
     column = lax.broadcasted_iota(jnp.int32, (LANES, LANES), 0).astype(F32).astype(BF16)
     channel = lax.broadcasted_iota(jnp.int32, (CP, LANES), 0).astype(F32)
     zero = jnp.zeros((LANES, LANES), BF16)
@@ -388,14 +425,14 @@
                 axis=0,
             )
             bsc[k] = table
-            return packet, dot(sobs[swath_ref[0, k]], table)
+            return packet, dot(sobs[patch_of(group, u)], table)
 
         def finish(u, given):
             k = group * GROUP + u
             packet, found = given
             picked = channel == packet[0:1]
             gap = jnp.sum(jnp.where(picked, found, 0.0), axis=0, keepdims=True) - packet[6:7]
-            inn[k] = gap
+            inn[k // pairs, lax.rem(k, pairs)] = gap
             qsc[k] = jnp.where(picked, packet[7:8] * gap, 0.0).astype(BF16)
 
         pipelined(range(GROUP), start, finish, LAG)
@@ -413,7 +450,7 @@
 
         def finish(u, share):
             k = group * GROUP + u
-            patch = swath_ref[0, k]
+            patch = patch_of(group, u)
             before = sum(jnp.where(patch == m, slots[-1][m], 0) for m in range(chunks))
             hist[k + 1] = hist[before] + share
             slots.append(tuple(jnp.where(patch == m, k + 1, slots[-1][m]) for m in range(chunks)))
@@ -422,12 +459,12 @@
         return slots[-1]
 
     last = lax.fori_loop(0, owners // GROUP, pull, (jnp.int32(0),) * chunks)
-    inn_recv[me] = inn[me]
+    inn_recv[:, my_pair] = inn[:, my_pair]
 
     def give_back(other, where):
         pltpu.make_async_remote_copy(
-            src_ref=inn.at[other], dst_ref=inn_recv.at[me], send_sem=isend, recv_sem=irecv,
-            device_id=where, device_id_type=MESH,
+            src_ref=inn.at[:, other], dst_ref=inn_recv.at[:, my_pair],
+            send_sem=isend, recv_sem=irecv, device_id=where, device_id_type=MESH,
         ).start()
 
     def tap(i, j, r):
@@ -454,11 +491,13 @@
         rounded = jnp.concatenate([cotangent.astype(BF16), jnp.zeros((LANES - CP, breadth), BF16)], axis=0)
         return (dot(wot_ref[...], rounded) * slope).astype(BF16)
 
-    def products(cotangent, slope):
+    def products(cotangent, slope, beside=None):
         def start(n):
             return spread_of(cotangent(n), slope[:, pl.ds(n * WIDE, WIDE)])
 
         def finish(n, spread):
+            if beside:
+                to_some(n, chunks, beside)
             for i in range(3):
                 ybuf[pl.ds(3 * i * CP, 3 * CP), pl.ds(n * WIDE, WIDE)] = dot(wk[i, pl.ds(0, 3 * CP), :], spread)
 
@@ -510,17 +549,15 @@
             inflow = inflow + jnp.where(lane == goes, rolled(value, goes - came), 0.0)
         return rrow[t, 0].astype(F32), rrow[t, 1].astype(F32), inflow
 
-    products(lambda n: hist[last[n]], slope2)
+    products(lambda n: hist[last[n]], slope2, give_back)
     columns = local_sums(0, lambda r: hist[last[r // 2]][:, (r % 2) * LANES : (r % 2 + 1) * LANES])
     send_rim(0, ubuf[0, :, block(1, -1)], ubuf[0, :, block(1, height)], columns)
 
-    to_some(0, 2, give_back)
     products(lambda n: ubuf[0, :, block(1, 2 * n, 2)], slope1)
     columns = local_sums(1, None)
     at_edge = jnp.zeros((CP, LANES), F32)
     for r in range(height):
         at_edge = gathered(at_edge, r, ubuf[0, :, block(1, r)])
-    to_some(1, 2, give_back)
     above, below, inflow = receive_rim(0)
     far = height - 1
     at_edge = at_edge + inflow
@@ -564,6 +601,15 @@
         ubuf[1, :, block(1, height)] + inner(*late_row(1, 1)) + from_columns(height, same),
         columns,
     )
+    pltpu.make_async_remote_copy(
+        src_ref=inn.at[:, others], dst_ref=inn_recv.at[:, others], send_sem=isend, recv_sem=irecv,
+        device_id=ids[RIGHT], device_id_type=MESH,
+    ).wait()
+    innov_to_mate = pltpu.make_async_remote_copy(
+        src_ref=inn_recv.at[1], dst_ref=inn_mate, send_sem=gsend.at[1], recv_sem=grecv.at[1],
+        device_id=mate, device_id_type=MESH,
+    )
+    innov_to_mate.start()
     outermost = same + inflow
     for r in range(height):
         value = ubuf[0, :, block(1, r)] + ubuf[1, :, block(1, r)] + from_columns(r, outermost)
@@ -586,12 +632,13 @@
         here = pl.ds(r, chan, stride=height)
         grad_ref[here, :] = grad_ref[here, :] + value[:chan]
 
-    rows = pl.ds(0, owners - 1)
-    pltpu.make_async_remote_copy(
-        src_ref=inn.at[rows], dst_ref=inn_recv.at[rows], send_sem=isend, recv_sem=irecv,
-        device_id=ids[RIGHT], device_id_type=MESH,
-    ).wait()
-    innov_ref[...] = inn_recv[...].reshape(owners, LANES)
+    innov_to_mate.wait()
+    to_mate.wait_send()
+    for h in range(halves):
+        part = pl.ds(h * n_lon, n_lon)
+        for which, ref in ((side, inn_recv.at[0]), (1 - side, inn_mate)):
+            rows = pl.ds(pl.multiple_of((2 * h + which) * n_lon, n_lon), n_lon)
+            innov_ref[rows, :] = ref[part].reshape(n_lon, LANES)
     for d in range(8):
         wait_send(state_sources[d], 0, d, fsend, frecv)
     for t in range(2):
@@ -652,8 +699,9 @@
             pltpu.VMEM((CP, hid), BF16),
             pltpu.VMEM((hid, LANES), BF16),
             pltpu.VMEM((CP * height, LANES), F32),
-            pltpu.VMEM((owners, 4, LANES), jnp.int32),
-            pltpu.VMEM((owners, 4, LANES), jnp.int32),
+            pltpu.VMEM((owners // 2, 4, LANES), jnp.int32),
+            pltpu.VMEM((2, owners // 2, 4, LANES), jnp.int32),
+            pltpu.VMEM((2, owners // 2, 4, LANES), jnp.int32),
             pltpu.VMEM((owners * 8, LANES), F32),
             pltpu.VMEM((hid, (height + 4) * LANES), BF16),
             pltpu.VMEM((hid, (height + 2) * LANES), BF16),
@@ -666,8 +714,9 @@
             pltpu.VMEM((6, CP, LANES), BF16),
             pltpu.VMEM((owners, WIDE, LANES), BF16),
             pltpu.VMEM((owners, CP, LANES), BF16),
-            pltpu.VMEM((owners, 1, LANES), F32),
-            pltpu.VMEM((owners, 1, LANES), F32),
+            pltpu.VMEM((2, owners // 2, 1, LANES), F32),
+            pltpu.VMEM((2, owners // 2, 1, LANES), F32),
+            pltpu.VMEM((owners // 2, 1, LANES), F32),
             pltpu.VMEM((owners + 1, CP, WIDE), F32),
             pltpu.VMEM((9 * CP, cells), F32),
             pltpu.VMEM((9 * CP, 3 * LANES), F32),
@@ -677,7 +726,7 @@
             pltpu.VMEM((2, 2, CP, LANES), BF16),
             pltpu.VMEM((2, 6, CP, LANES), BF16),
             dma((1, 8)), dma((1, 8)), dma((2, 8)), dma((2, 8)),
-            dma, dma, dma, dma, dma((6,)),
+            dma, dma, dma, dma, dma((2,)), dma((2,)), dma((6,)),
         ],
         compiler_params=pltpu.CompilerParams(
             collective_id=0, has_side_effects=True, vmem_limit_bytes=56 * 1024 * 1024

time: 48.4 us -> 47.1 us (0.973)
  Pallas kernels: 47.4 us -> 46.1 us
    pallas_call x1, Pallas kernels: 45.6 us -> 44.2 us  [local(): pl.pallas_call(functools.partial(kernel, n_lat, n_lon, hid), out_shape=(j...]
where the time goes in v6:
time: 47.1 us; the launch traced here: 46.9 us
  Pallas kernels  46.1 us (98%)
  between operations  0.8 us (2%)
    pallas_call x1, Pallas kernels, local(): pl.pallas_call(functools.partial(kernel, n_lat, n_lon, hid), out_shape=(j...  44.2 us
    pallas_call x1, Pallas kernels, local(): pl.pallas_call(hand_over, out_shape=(jax.ShapeDtypeStruct((chan, height,...  1.87 us

profile of v6, /device:TPU:1, one launch (start us, length us, event | category | flops | bytes accessed | tf_op | source)
XLA Modules:
  0.0 46.9 jit_solution(15521746971936649805)
XLA Ops:
  0.6 44.2 %shard_map.122 = (f32[1104,128]{1,0:T(8,128)}, f32[128,128]{1,0:T(8,128)}) custom-call(bf16[69,16,128]{2,1,0:T(8,128)(2,1)} %x_hbm.1, bf16[69,16,128]{2,1,0:T(8,128)(2,1)} %xb_hbm.1, f32[1,69]{1,0:T(1,128)} %bitcast.15, bf16[9,69,256]{2,1,0:T(8,128)(2,1)} %cw_ref.1, f32[1,256]{1,0:T(1,128)} %bitcast.14, bf16[69,256]{1,0:T(8,128)(2,1)} %ow_ref.1, ...), custom_call_target="tpu_custom_call" | custom-call | tf_op jit(solution)/shard_map/pallas_call | solution.py:681
  44.9 1.9 %shard_map.123 = (f32[69,16,128]{2,1,0:T(8,128)}, f32[1,128,128]{2,1,0:T(8,128)}) custom-call(f32[69,16,128]{2,1,0:T(8,128)} %bitcast.8, f32[1,128,128]{2,1,0:T(8,128)} %bitcast.13), custom_call_target="tpu_custom_call" | custom-call | tf_op jit(solution)/shard_map/pallas_call | solution.py:738

commit v7 on v6

--- a/solution.py
+++ b/solution.py
@@ -491,13 +491,11 @@
         rounded = jnp.concatenate([cotangent.astype(BF16), jnp.zeros((LANES - CP, breadth), BF16)], axis=0)
         return (dot(wot_ref[...], rounded) * slope).astype(BF16)
 
-    def products(cotangent, slope, beside=None):
+    def products(cotangent, slope):
         def start(n):
             return spread_of(cotangent(n), slope[:, pl.ds(n * WIDE, WIDE)])
 
         def finish(n, spread):
-            if beside:
-                to_some(n, chunks, beside)
             for i in range(3):
                 ybuf[pl.ds(3 * i * CP, 3 * CP), pl.ds(n * WIDE, WIDE)] = dot(wk[i, pl.ds(0, 3 * CP), :], spread)
 
@@ -549,10 +547,11 @@
             inflow = inflow + jnp.where(lane == goes, rolled(value, goes - came), 0.0)
         return rrow[t, 0].astype(F32), rrow[t, 1].astype(F32), inflow
 
-    products(lambda n: hist[last[n]], slope2, give_back)
+    products(lambda n: hist[last[n]], slope2)
     columns = local_sums(0, lambda r: hist[last[r // 2]][:, (r % 2) * LANES : (r % 2 + 1) * LANES])
     send_rim(0, ubuf[0, :, block(1, -1)], ubuf[0, :, block(1, height)], columns)
 
+    to_some(0, 1, give_back)
     products(lambda n: ubuf[0, :, block(1, 2 * n, 2)], slope1)
     columns = local_sums(1, None)
     at_edge = jnp.zeros((CP, LANES), F32)

time: 47.1 us -> 45.8 us (0.972)
  Pallas kernels: 46.1 us -> 45 us
    pallas_call x1, Pallas kernels: 44.2 us -> 43.1 us  [local(): pl.pallas_call(functools.partial(kernel, n_lat, n_lon, hid), out_shape=(j...]
where the time goes in v7:
time: 45.8 us; the launch traced here: 45.6 us
  Pallas kernels  45 us (98%)
  between operations  0.64 us (1%)
    pallas_call x1, Pallas kernels, local(): pl.pallas_call(functools.partial(kernel, n_lat, n_lon, hid), out_shape=(j...  43.1 us
    pallas_call x1, Pallas kernels, local(): pl.pallas_call(hand_over, out_shape=(jax.ShapeDtypeStruct((chan, height,...  1.87 us

profile of v7, /device:TPU:1, one launch (start us, length us, event | category | flops | bytes accessed | tf_op | source)
XLA Modules:
  0.0 45.6 jit_solution(7648686325077326862)
XLA Ops:
  0.6 43.1 %shard_map.122 = (f32[1104,128]{1,0:T(8,128)}, f32[128,128]{1,0:T(8,128)}) custom-call(bf16[69,16,128]{2,1,0:T(8,128)(2,1)} %x_hbm.1, bf16[69,16,128]{2,1,0:T(8,128)(2,1)} %xb_hbm.1, f32[1,69]{1,0:T(1,128)} %bitcast.15, bf16[9,69,256]{2,1,0:T(8,128)(2,1)} %cw_ref.1, f32[1,256]{1,0:T(1,128)} %bitcast.14, bf16[69,256]{1,0:T(8,128)(2,1)} %ow_ref.1, ...), custom_call_target="tpu_custom_call" | custom-call | tf_op jit(solution)/shard_map/pallas_call | solution.py:680
  43.8 1.9 %shard_map.123 = (f32[69,16,128]{2,1,0:T(8,128)}, f32[1,128,128]{2,1,0:T(8,128)}) custom-call(f32[69,16,128]{2,1,0:T(8,128)} %bitcast.8, f32[1,128,128]{2,1,0:T(8,128)} %bitcast.13), custom_call_target="tpu_custom_call" | custom-call | tf_op jit(solution)/shard_map/pallas_call | solution.py:737

commit v8 on v7

--- a/solution.py
+++ b/solution.py
@@ -38,7 +38,7 @@
     n_lat, n_lon, hid,
     x_hbm, xb_hbm, bp_ref, cw_ref, cb_ref, ow_ref, swath_ref, cell_hbm, w_hbm, val_hbm, prec_hbm,
     grad_ref, innov_ref,
-    x_ref, xb_ref, cell_ref, w_ref, val_ref, prec_ref, wpad, wk, wt_ref, wo_ref, wot_ref, x32, given, packed, recv, opened, s1, s2, se, sobs, slope1, slope2, slope_edge, csend, hcol,
+    x_ref, xb_ref, cell_ref, w_ref, val_ref, prec_ref, wpad, wk, wt_ref, wo_ref, wot_ref, x32, given, packed, recv, opened, s1, s2, se, sobs, slope1, slope2, slope_edge, slope_edge2, csend, hcol,
     bsc, qsc, inn, inn_recv, inn_mate, hist, ybuf, xbuf, ubuf, brow, bcol, rrow, rcol,
     fsend, frecv, bsend, brecv, psend, precv, isend, irecv, gsend, grecv, loaded,
 ):
@@ -262,6 +262,10 @@
                 held.append(start(order[k + lag]))
             finish(n, held.pop(0))
 
+    def kept_cells():
+        here = lax.rem(lane_iota(hid), LANES // 2)
+        return jnp.logical_and(lax.rem(here, 2) == 0, jnp.logical_and(here >= spot(0), here <= spot(height - 1)))
+
     def first_rim(centre):
         up, down = has_up.astype(F32), has_down.astype(F32)
         rows = (-1, height)
@@ -274,9 +278,7 @@
         sides, tangent = network(conv(lambda i: se[i]), centre)
         place = lax.rem(lane, LANES // 2)
         inside = jnp.where(place == spot(-1), up, jnp.where(place == spot(height), down, 1.0))
-        here = lax.rem(lane_iota(hid), LANES // 2)
-        kept = jnp.logical_and(lax.rem(here, 2) == 0, jnp.logical_and(here >= spot(0), here <= spot(height - 1)))
-        slope_edge[...] = jnp.where(kept, tangent()[:, LANES:], 0.0)
+        slope_edge[...] = jnp.where(kept_cells(), tangent()[:, LANES:], 0.0)
         return tuple((sides[:, k * LANES : (k + 1) * LANES] * inside).astype(BF16).astype(F32) for k in (0, 1))
 
     pl.semaphore_wait(barrier, pairs - 1 + 3 * (has_up.astype(jnp.int32) + has_down.astype(jnp.int32)))
@@ -371,6 +373,12 @@
         sobs[n] = forward_chunk(pre, s2, 1, n, slope2, False)
 
     pipelined(range(chunks), lambda n: conv_chunk(s2, 1, n), second_step)
+    hid_lane = lane_iota(hid)
+    tangents = jnp.zeros((hid, LANES), F32)
+    for r in range(height):
+        tangents = jnp.where((hid_lane + 1) // 2 == r + 2, rolled(slope2[:, block(0, r)], spot(r)), tangents)
+    tangents = jnp.where(hid_lane < LANES // 2, tangents, rolled(tangents, LANES // 2 + 1))
+    slope_edge2[...] = jnp.where(kept_cells(), tangents, 0.0)
 
     others = pl.ds(0, pairs - 1)
     pltpu.make_async_remote_copy(
@@ -508,12 +516,15 @@
             + jnp.where(last_lane, 0.0, rolled(t_low, -1))
         )
 
-    def local_sums(t, own):
+    def own_sums(own):
+        for r in range(height):
+            ubuf[0, :, block(1, r)] = inner(*(summed(j, r) for j in (-1, 0, 1))) + own(r)
+
+    def local_sums(t):
         columns = jnp.zeros((CP, LANES), F32)
         for r in range(-1, height + 1):
             t_low, t_mid, t_high = (summed(j, r) for j in (-1, 0, 1))
-            total = inner(t_low, t_mid, t_high)
-            ubuf[t, :, block(1, r)] = total + own(r) if 0 <= r < height and own else total
+            ubuf[t, :, block(1, r)] = inner(t_low, t_mid, t_high)
             columns = gathered(columns, r, jnp.where(first_lane, t_low, t_high))
         return columns
 
@@ -547,40 +558,59 @@
             inflow = inflow + jnp.where(lane == goes, rolled(value, goes - came), 0.0)
         return rrow[t, 0].astype(F32), rrow[t, 1].astype(F32), inflow
 
+    far = height - 1
+    outside = slot_of <= height + 2
+
+    def rim_products(top_row, bottom_row, at_edge, slopes):
+        late = spread_of(
+            jnp.concatenate([top_row, bottom_row, apart(at_edge)], axis=1), jnp.concatenate(slopes, axis=1)
+        )
+        for i in range(3):
+            xbuf[pl.ds(3 * i * CP, 3 * CP), :] = dot(wk[i, pl.ds(0, 3 * CP), :], late)
+
+    def late_tap(i, j, part):
+        return xbuf[pl.ds((3 * (i + 1) + j + 1) * CP, CP), pl.ds(part * LANES, LANES)]
+
+    def late_row(part, i):
+        return tuple(late_tap(i, j, part) for j in (-1, 0, 1))
+
+    def late_columns(j):
+        return sum(rolled(late_tap(i, j, 2), 2 * i) for i in (-1, 0, 1))
+
+    def outward(to_low, to_high):
+        return jnp.where(outside, jnp.where(even, to_low, rolled(to_high, -LANES // 2 - 1)), 0.0)
+
+    def pull_row(r):
+        return hist[last[r // 2]][:, (r % 2) * LANES : (r % 2 + 1) * LANES]
+
+    at_edge = jnp.zeros((CP, LANES), F32)
+    for r in range(height):
+        at_edge = gathered(at_edge, r, pull_row(r))
+    rim_products(
+        pull_row(0), pull_row(far), at_edge,
+        [slope2[:, pl.ds(0, LANES)], slope2[:, pl.ds(far * LANES, LANES)], slope_edge2[...]],
+    )
+    send_rim(
+        0, inner(*late_row(0, -1)), inner(*late_row(1, 1)), outward(late_columns(-1), late_columns(1))
+    )
     products(lambda n: hist[last[n]], slope2)
-    columns = local_sums(0, lambda r: hist[last[r // 2]][:, (r % 2) * LANES : (r % 2 + 1) * LANES])
-    send_rim(0, ubuf[0, :, block(1, -1)], ubuf[0, :, block(1, height)], columns)
+    own_sums(pull_row)
 
     to_some(0, 1, give_back)
     products(lambda n: ubuf[0, :, block(1, 2 * n, 2)], slope1)
-    columns = local_sums(1, None)
+    columns = local_sums(1)
     at_edge = jnp.zeros((CP, LANES), F32)
     for r in range(height):
         at_edge = gathered(at_edge, r, ubuf[0, :, block(1, r)])
     above, below, inflow = receive_rim(0)
-    far = height - 1
     at_edge = at_edge + inflow
     at_edge = at_edge + gathered(gathered(jnp.zeros((CP, LANES), F32), 0, above), far, below)
-    late = spread_of(
-        jnp.concatenate([above, below, apart(at_edge)], axis=1),
-        jnp.concatenate(
-            [slope1[:, pl.ds(0, LANES)], slope1[:, pl.ds(far * LANES, LANES)], slope_edge[...]], axis=1
-        ),
-    )
-    for i in range(3):
-        xbuf[pl.ds(3 * i * CP, 3 * CP), :] = dot(wk[i, pl.ds(0, 3 * CP), :], late)
-
-    def late_tap(i, j, part):
-        return xbuf[pl.ds((3 * (i + 1) + j + 1) * CP, CP), pl.ds(part * LANES, LANES)]
-
-    def late_row(part, i):
-        return tuple(late_tap(i, j, part) for j in (-1, 0, 1))
-
-    to_low, to_same, to_high = (
-        sum(rolled(late_tap(i, j, 2), 2 * i) for i in (-1, 0, 1)) for j in (-1, 0, 1)
-    )
-    outside = slot_of <= height + 2
-    columns = columns + jnp.where(outside, jnp.where(even, to_low, rolled(to_high, -LANES // 2 - 1)), 0.0)
+    rim_products(
+        above, below, at_edge,
+        [slope1[:, pl.ds(0, LANES)], slope1[:, pl.ds(far * LANES, LANES)], slope_edge[...]],
+    )
+    to_low, to_same, to_high = (late_columns(j) for j in (-1, 0, 1))
+    columns = columns + outward(to_low, to_high)
     for part, base in ((0, 0), (1, far)):
         for i in (-1, 0, 1):
             t_low, _, t_high = late_row(part, i)
@@ -709,6 +739,7 @@
             pltpu.VMEM((hid, cells), F32),
             pltpu.VMEM((hid, cells), F32),
             pltpu.VMEM((hid, LANES), F32),
+            pltpu.VMEM((hid, LANES), F32),
             pltpu.VMEM((2, CP, LANES), BF16),
             pltpu.VMEM((6, CP, LANES), BF16),
             pltpu.VMEM((owners, WIDE, LANES), BF16),

time: 45.8 us -> 45 us (0.983)
  Pallas kernels: 45 us -> 44 us
    pallas_call x1, Pallas kernels: 43.1 us -> 42.1 us  [local(): pl.pallas_call(functools.partial(kernel, n_lat, n_lon, hid), out_shape=(j...]
where the time goes in v8:
time: 45 us; the launch traced here: 44.8 us
  Pallas kernels  44 us (98%)
  between operations  0.8 us (2%)
    pallas_call x1, Pallas kernels, local(): pl.pallas_call(functools.partial(kernel, n_lat, n_lon, hid), out_shape=(j...  42.1 us
    pallas_call x1, Pallas kernels, local(): pl.pallas_call(hand_over, out_shape=(jax.ShapeDtypeStruct((chan, height,...  1.87 us

profile of v8, /device:TPU:1, one launch (start us, length us, event | category | flops | bytes accessed | tf_op | source)
XLA Modules:
  0.0 44.8 jit_solution(9832320943587135759)
XLA Ops:
  0.6 42.1 %shard_map.122 = (f32[1104,128]{1,0:T(8,128)}, f32[128,128]{1,0:T(8,128)}) custom-call(bf16[69,16,128]{2,1,0:T(8,128)(2,1)} %x_hbm.1, bf16[69,16,128]{2,1,0:T(8,128)(2,1)} %xb_hbm.1, f32[1,69]{1,0:T(1,128)} %bitcast.15, bf16[9,69,256]{2,1,0:T(8,128)(2,1)} %cw_ref.1, f32[1,256]{1,0:T(1,128)} %bitcast.14, bf16[69,256]{1,0:T(8,128)(2,1)} %ow_ref.1, ...), custom_call_target="tpu_custom_call" | custom-call | tf_op jit(solution)/shard_map/pallas_call | solution.py:710
  42.8 1.9 %shard_map.123 = (f32[69,16,128]{2,1,0:T(8,128)}, f32[1,128,128]{2,1,0:T(8,128)}) custom-call(f32[69,16,128]{2,1,0:T(8,128)} %bitcast.8, f32[1,128,128]{2,1,0:T(8,128)} %bitcast.13), custom_call_target="tpu_custom_call" | custom-call | tf_op jit(solution)/shard_map/pallas_call | solution.py:768

commit v9 on v8

--- a/solution.py
+++ b/solution.py
@@ -18,7 +18,7 @@
 UP, DOWN, LEFT, RIGHT, UL, UR, DL, DR = range(8)
 GROUP = 32
 LAG = 3
-PIECES = 3
+PIECES = 2
 WORD = 65536
 HALF_WORD = 32768
 HALF_WORDS = 65535.0
@@ -533,18 +533,29 @@
         brow[t, 1] = below.astype(BF16)
         bcol[t] = columns.astype(BF16)
         src, dst = rim_sources(t), rim_targets(t)
-        for d in (UP, DOWN, LEFT, RIGHT, UL, UR, DL, DR):
+        for d in (LEFT, RIGHT, UL, UR, DL, DR, UP, DOWN):
             send(src[d], dst[opposite[d]], t, d, bsend, brecv)
 
-    def receive_rim(t):
+    def receive_rows(t):
         dst = rim_targets(t)
-        for d in range(8):
+        for d in (UP, DOWN):
             wait_recv(dst[d], t, d, bsend, brecv)
-        for there, row, slots in ((has_up, 0, (2, 3)), (has_down, 1, (4, 5))):
+        for there, row in ((has_up, 0), (has_down, 1)):
 
             @pl.when(jnp.logical_not(there))
             def _():
                 rrow[t, row] = jnp.zeros((CP, LANES), BF16)
+
+        return rrow[t, 0].astype(F32), rrow[t, 1].astype(F32)
+
+    def receive_columns(t):
+        dst = rim_targets(t)
+        for d in (LEFT, RIGHT, UL, UR, DL, DR):
+            wait_recv(dst[d], t, d, bsend, brecv)
+        for there, slots in ((has_up, (2, 3)), (has_down, (4, 5))):
+
+            @pl.when(jnp.logical_not(there))
+            def _():
                 for slot in slots:
                     rcol[t, slot] = jnp.zeros((CP, LANES), BF16)
 
@@ -556,17 +567,17 @@
             (ul, past - 1, top), (ur, past, top - 1), (dl, before - 1, bottom), (dr, before, bottom - 1),
         ):
             inflow = inflow + jnp.where(lane == goes, rolled(value, goes - came), 0.0)
-        return rrow[t, 0].astype(F32), rrow[t, 1].astype(F32), inflow
+        return inflow
 
     far = height - 1
     outside = slot_of <= height + 2
 
-    def rim_products(top_row, bottom_row, at_edge, slopes):
-        late = spread_of(
-            jnp.concatenate([top_row, bottom_row, apart(at_edge)], axis=1), jnp.concatenate(slopes, axis=1)
-        )
+    def rim_products(first_part, cells, slopes):
+        late = spread_of(jnp.concatenate(cells, axis=1), jnp.concatenate(slopes, axis=1))
         for i in range(3):
-            xbuf[pl.ds(3 * i * CP, 3 * CP), :] = dot(wk[i, pl.ds(0, 3 * CP), :], late)
+            xbuf[pl.ds(3 * i * CP, 3 * CP), pl.ds(first_part * LANES, late.shape[1])] = dot(
+                wk[i, pl.ds(0, 3 * CP), :], late
+            )
 
     def late_tap(i, j, part):
         return xbuf[pl.ds((3 * (i + 1) + j + 1) * CP, CP), pl.ds(part * LANES, LANES)]
@@ -587,7 +598,7 @@
     for r in range(height):
         at_edge = gathered(at_edge, r, pull_row(r))
     rim_products(
-        pull_row(0), pull_row(far), at_edge,
+        0, [pull_row(0), pull_row(far), apart(at_edge)],
         [slope2[:, pl.ds(0, LANES)], slope2[:, pl.ds(far * LANES, LANES)], slope_edge2[...]],
     )
     send_rim(
@@ -602,21 +613,20 @@
     at_edge = jnp.zeros((CP, LANES), F32)
     for r in range(height):
         at_edge = gathered(at_edge, r, ubuf[0, :, block(1, r)])
-    above, below, inflow = receive_rim(0)
-    at_edge = at_edge + inflow
-    at_edge = at_edge + gathered(gathered(jnp.zeros((CP, LANES), F32), 0, above), far, below)
-    rim_products(
-        above, below, at_edge,
-        [slope1[:, pl.ds(0, LANES)], slope1[:, pl.ds(far * LANES, LANES)], slope_edge[...]],
-    )
-    to_low, to_same, to_high = (late_columns(j) for j in (-1, 0, 1))
-    columns = columns + outward(to_low, to_high)
+    above, below = receive_rows(0)
+    rim_products(0, [above, below], [slope1[:, pl.ds(0, LANES)], slope1[:, pl.ds(far * LANES, LANES)]])
     for part, base in ((0, 0), (1, far)):
         for i in (-1, 0, 1):
             t_low, _, t_high = late_row(part, i)
             columns = columns + gathered(
                 jnp.zeros((CP, LANES), F32), base + i, jnp.where(first_lane, t_low, t_high)
             )
+    at_edge = at_edge + gathered(gathered(jnp.zeros((CP, LANES), F32), 0, above), far, below)
+    inflow = receive_columns(0)
+    at_edge = at_edge + inflow
+    rim_products(2, [apart(at_edge)], [slope_edge[...]])
+    to_low, to_same, to_high = (late_columns(j) for j in (-1, 0, 1))
+    columns = columns + outward(to_low, to_high)
     same = joined(to_same)
     next_in = jnp.where(even, rolled(to_low, -LANES // 2 - 2), rolled(to_high, 1))
     second = jnp.logical_or(lane == 1, lane == LANES - 2)
@@ -651,7 +661,8 @@
         if r == far:
             value = value + below
         ubuf[0, :, block(1, r)] = value
-    above, below, inflow = receive_rim(1)
+    above, below = receive_rows(1)
+    inflow = receive_columns(1)
     for r in range(height):
         value = ubuf[0, :, block(1, r)] + jnp.where(edge, rolled(inflow, -spot(r)), 0.0)
         if r == 0:

time: 45 us -> 45 us (level)
  no operation moved by 1% of the time
where the time goes in v9:
time: 45 us; the launch traced here: 44.8 us
  Pallas kernels  44 us (98%)
  between operations  0.8 us (2%)
    pallas_call x1, Pallas kernels, local(): pl.pallas_call(functools.partial(kernel, n_lat, n_lon, hid), out_shape=(j...  42.2 us
    pallas_call x1, Pallas kernels, local(): pl.pallas_call(hand_over, out_shape=(jax.ShapeDtypeStruct((chan, height,...  1.82 us

profile of v9, /device:TPU:1, one launch (start us, length us, event | category | flops | bytes accessed | tf_op | source)
XLA Modules:
  0.0 44.8 jit_solution(12617688917506731987)
XLA Ops:
  0.6 42.2 %shard_map.122 = (f32[1104,128]{1,0:T(8,128)}, f32[128,128]{1,0:T(8,128)}) custom-call(bf16[69,16,128]{2,1,0:T(8,128)(2,1)} %x_hbm.1, bf16[69,16,128]{2,1,0:T(8,128)(2,1)} %xb_hbm.1, f32[1,69]{1,0:T(1,128)} %bitcast.15, bf16[9,69,256]{2,1,0:T(8,128)(2,1)} %cw_ref.1, f32[1,256]{1,0:T(1,128)} %bitcast.14, bf16[69,256]{1,0:T(8,128)(2,1)} %ow_ref.1, ...), custom_call_target="tpu_custom_call" | custom-call | tf_op jit(solution)/shard_map/pallas_call | solution.py:721
  42.8 1.8 %shard_map.123 = (f32[69,16,128]{2,1,0:T(8,128)}, f32[1,128,128]{2,1,0:T(8,128)}) custom-call(f32[69,16,128]{2,1,0:T(8,128)} %bitcast.8, f32[1,128,128]{2,1,0:T(8,128)} %bitcast.13), custom_call_target="tpu_custom_call" | custom-call | tf_op jit(solution)/shard_map/pallas_call | solution.py:779

commit v10 on v9

--- a/solution.py
+++ b/solution.py
@@ -334,6 +334,7 @@
     wpad[pl.ds(0, chan), :] = ow_ref[...].astype(F32)
     wo_ref[...] = wpad[pl.ds(0, CP), :].astype(BF16)
     wot_ref[...] = jnp.transpose(wpad[...]).astype(BF16)
+    grad_ref[pl.ds(chan * height, (CP - chan) * height), :] = jnp.zeros(((CP - chan) * height, LANES), F32)
     for c in range(chan):
         grad_ref[pl.ds(c * height, height), :] = bp_ref[0, c] * (x_ref[c].astype(F32) - xb_ref[c].astype(F32))
 
@@ -669,8 +670,8 @@
             value = value + above
         if r == far:
             value = value + below
-        here = pl.ds(r, chan, stride=height)
-        grad_ref[here, :] = grad_ref[here, :] + value[:chan]
+        here = pl.ds(r, CP, stride=height)
+        grad_ref[here, :] = grad_ref[here, :] + value
 
     innov_to_mate.wait()
     to_mate.wait_send()
@@ -688,7 +689,7 @@
 
 
 def hand_over(gradient_in, innov_in, gradient_out, innov_out, gradient_held, innov_held, sems):
-    chan = gradient_in.shape[0]
+    chan = gradient_out.shape[0]
     cuts = [chan * k // PIECES for k in range(PIECES + 1)]
     parts = [pl.ds(a, b - a) for a, b in zip(cuts, cuts[1:])]
     routes = [(gradient_in.at[p], gradient_held.at[p], gradient_out.at[p]) for p in parts]
@@ -721,7 +722,7 @@
     gradient, innov = pl.pallas_call(
         functools.partial(kernel, n_lat, n_lon, hid),
         out_shape=(
-            jax.ShapeDtypeStruct((chan * height, LANES), F32),
+            jax.ShapeDtypeStruct((CP * height, LANES), F32),
             jax.ShapeDtypeStruct((owners, LANES), F32),
         ),
         in_specs=[hbm, hbm, smem, vmem, vmem, vmem, smem] + [hbm] * 4,
@@ -790,7 +791,7 @@
             dma((2, PIECES + 1)),
         ],
         compiler_params=pltpu.CompilerParams(vmem_limit_bytes=56 * 1024 * 1024),
-    )(gradient.reshape(chan, height, breadth), innov[None])
+    )(gradient.reshape(CP, height, breadth), innov[None])
 
 
 def solution(mesh):

time: 45 us -> 45 us (level)
  no operation moved by 1% of the time
where the time goes in v10:
time: 45 us; the launch traced here: 44.9 us
  Pallas kernels  44.1 us (98%)
  between operations  0.8 us (2%)
    pallas_call x1, Pallas kernels, local(): pl.pallas_call(functools.partial(kernel, n_lat, n_lon, hid), out_shape=(j...  42.2 us
    pallas_call x1, Pallas kernels, local(): pl.pallas_call(hand_over, out_shape=(jax.ShapeDtypeStruct((chan, height,...  1.82 us

profile of v10, /device:TPU:1, one launch (start us, length us, event | category | flops | bytes accessed | tf_op | source)
XLA Modules:
  0.0 44.9 jit_solution(11375444479723458494)
XLA Ops:
  0.6 42.2 %shard_map.122 = (f32[1280,128]{1,0:T(8,128)}, f32[128,128]{1,0:T(8,128)}) custom-call(bf16[69,16,128]{2,1,0:T(8,128)(2,1)} %x_hbm.1, bf16[69,16,128]{2,1,0:T(8,128)(2,1)} %xb_hbm.1, f32[1,69]{1,0:T(1,128)} %bitcast.15, bf16[9,69,256]{2,1,0:T(8,128)(2,1)} %cw_ref.1, f32[1,256]{1,0:T(1,128)} %bitcast.14, bf16[69,256]{1,0:T(8,128)(2,1)} %ow_ref.1, ...), custom_call_target="tpu_custom_call" | custom-call | tf_op jit(solution)/shard_map/pallas_call | solution.py:722
  42.9 1.8 %shard_map.123 = (f32[69,16,128]{2,1,0:T(8,128)}, f32[1,128,128]{2,1,0:T(8,128)}) custom-call(f32[80,16,128]{2,1,0:T(8,128)} %bitcast.8, f32[1,128,128]{2,1,0:T(8,128)} %bitcast.13), custom_call_target="tpu_custom_call" | custom-call | tf_op jit(solution)/shard_map/pallas_call | solution.py:780
